TPU v7x, 32 devices: a whole 2x2x4 slice. The times are simulated.
32 devices in a mesh: grp: 2 (over y), row: 4 (over z), col: 4 (over x, core).
Axes of the slice: x: 2, y: 2, z: 4, core: 2. Of those that a mesh axis runs over, the one named last changes fastest.
Arguments:
- pair_track: bfloat16 [64, 32, 128], P(('grp', 'row'), 'col'), parts along dimension 0, may hold values from -6 to 6
- pair_mask: int32 [64, 32], P(('grp', 'row'), 'col'), parts along dimension 0, may hold values from 0 to 1, as said below
- token_mask: int32 [64], P('grp'), parts along dimension 0, may hold values from 0 to 1, as said below
- mult_gate: bfloat16 [128, 256], replicated, may hold values from -0.5 to 0.5
- mult_value: bfloat16 [128, 256], replicated, may hold values from -0.5 to 0.5
- mult_outgate: bfloat16 [128, 128], replicated, may hold values from -0.5 to 0.5
- mult_outproj: bfloat16 [128, 128], replicated, may hold values from -0.5 to 0.5
- attn_proj: bfloat16 [128, 512], replicated, may hold values from -0.5 to 0.5
- attn_bias: bfloat16 [128, 4], replicated, may hold values from -44 to 44
- attn_outproj: bfloat16 [128, 128], replicated, may hold values from -0.5 to 0.5
- trans_gate: bfloat16 [128, 512], replicated, may hold values from -0.5 to 0.5
- trans_value: bfloat16 [128, 512], replicated, may hold values from -0.5 to 0.5
- trans_outproj: bfloat16 [512, 128], replicated, may hold values from -0.25 to 0.25
Outputs:
- pair_out: bfloat16 [64, 32, 128], P(('grp', 'row', 'col')), parts along dimension 0
There are 2 independent parts, one for each index of `grp`. A program takes and returns all parts, laid end to end along the dimension named above; an argument that names none is the same for every part. Nothing has to cross between parts.
Inputs may be any that keep to these rules, and one draw needn't show every extreme that they name: pair_mask[i, 0] and pair_mask[i, i] are 1 for every i. token_mask is 1 on a leading run of at least 24 tokens and 0 after it; at least the last token is 0.
All inputs are finite; a program needn't handle non-finite values.
Results may differ from a plain program's by a relative error of at most 0.015.
The roundings to bfloat16 on the way count: a program that leaves them out, or rounds other values in their place, can miss the bound.
Values may be sent and summed in bfloat16 or wider, within the bound.
No kernel may reach another device: no remote copies, remote signals or barrier semaphores. Data moves between devices by JAX's collectives and lax.ppermute only.
A program may use at most 64 MiB of HBM per device.

v0:
```python
import jax
import jax.numpy as jnp
from jax import lax
from jax.sharding import PartitionSpec as P

epsilon = 1e-05
masked_score = -1000000000.0


def normalize(values, axis):
    widened = values.astype(jnp.float32)
    center = widened - jnp.mean(widened, axis=axis, keepdims=True)
    spread = jnp.mean(center * center, axis=axis, keepdims=True)
    return center * lax.rsqrt(spread + epsilon)


def project(normed, weight):
    return jnp.einsum("rkc,cd->rkd", normed, weight, preferred_element_type=jnp.float32)


def on_device(
    pair_track,
    pair_mask,
    token_mask,
    mult_gate,
    mult_value,
    mult_outgate,
    mult_outproj,
    attn_proj,
    attn_bias,
    attn_outproj,
    trans_gate,
    trans_value,
    trans_outproj,
):
    col_count = lax.axis_size("col")
    rows_here = pair_track.shape[0] // col_count
    full_rows, full_mask = (
        lax.all_to_all(pair_track, "col", split_axis=0, concat_axis=1, tiled=True),
        lax.all_to_all(
            pair_mask.astype(jnp.bfloat16), "col", split_axis=0, concat_axis=1, tiled=True
        ),
    )
    length = full_rows.shape[1]
    row_start = (lax.axis_index("row") * col_count + lax.axis_index("col")) * rows_here
    token_rows = token_mask.astype(jnp.float32)
    own_tokens = lax.dynamic_slice_in_dim(token_rows, row_start, rows_here, 0)
    key_mask = full_mask.astype(jnp.float32) * token_rows[None, :]
    mult_mask = key_mask * own_tokens[:, None]
    residual = full_rows.astype(jnp.float32)
    normed = normalize(full_rows, 2).astype(jnp.bfloat16)
    gate_logit = jnp.einsum("rkc,cd->drk", normed, mult_gate, preferred_element_type=jnp.float32)
    value_part = jnp.einsum("rkc,cd->drk", normed, mult_value, preferred_element_type=jnp.float32)
    hidden = mult_gate.shape[1] // 2
    paired = (jax.nn.sigmoid(gate_logit) * value_part * mult_mask[None]).astype(jnp.bfloat16)
    paired = paired.reshape(2, hidden, rows_here, length)
    spread_pair = lax.all_to_all(paired, "col", split_axis=1, concat_axis=2, tiled=True)
    left_side = spread_pair[0]
    crossed = jnp.einsum(
        "cik,cjk->cij",
        left_side,
        lax.all_gather(spread_pair[1], "row", axis=1, tiled=True),
        preferred_element_type=jnp.float32,
    )
    crossed = crossed.astype(jnp.bfloat16)
    merged = lax.all_to_all(crossed, "col", split_axis=1, concat_axis=0, tiled=True)
    mixed_norm = normalize(merged, 0).astype(jnp.bfloat16)
    update = jnp.einsum("crk,cd->rkd", mixed_norm, mult_outproj, preferred_element_type=jnp.float32)
    outgate = jax.nn.sigmoid(project(normed, mult_outgate))
    residual = residual + outgate * update
    normed = normalize(residual, 2).astype(jnp.bfloat16)
    head_count = attn_bias.shape[1]
    inner_width = attn_outproj.shape[0]
    head_width = inner_width // head_count
    projected = project(normed, attn_proj)
    queries = (projected[:, :, :inner_width] * head_width ** (-0.5)).astype(jnp.bfloat16)
    queries = queries.reshape(rows_here, length, head_count, head_width)
    key_rows = (
        projected[:, :, inner_width : 2 * inner_width]
        .astype(jnp.bfloat16)
        .reshape(rows_here, length, head_count, head_width)
    )
    value_rows = (
        projected[:, :, 2 * inner_width : 3 * inner_width]
        .astype(jnp.bfloat16)
        .reshape(rows_here, length, head_count, head_width)
    )
    gating = jax.nn.sigmoid(projected[:, :, 3 * inner_width :])
    bias_local = jnp.einsum(
        "rkc,ch->hrk", normed, attn_bias, preferred_element_type=jnp.float32
    ).astype(jnp.bfloat16)
    allowed = key_mask > 0.5
    segment = lax.all_gather(bias_local, ("row", "col"), axis=1, tiled=True)
    amount = segment.shape[1]
    scores = jnp.einsum("rjhd,rkhd->hrjk", queries, key_rows, preferred_element_type=jnp.float32)
    scores = scores + segment.astype(jnp.float32)[:, None]
    scores = jnp.where(allowed[None, :, None, :], scores, masked_score)
    row_max = jnp.max(scores, axis=3, keepdims=True)
    expo = jnp.exp(scores - row_max)
    attn_weights = (expo / jnp.sum(expo, axis=3, keepdims=True)).astype(jnp.bfloat16)
    mixed_heads = jnp.einsum(
        "hrjk,rkhd->rjhd", attn_weights, value_rows, preferred_element_type=jnp.float32
    )
    gated_out = (gating * mixed_heads.reshape(rows_here, amount, inner_width)).astype(jnp.bfloat16)
    attended = jnp.einsum(
        "rjd,dc->rjc", gated_out, attn_outproj, preferred_element_type=jnp.float32
    )
    residual = residual + attended
    normed = normalize(residual, 2).astype(jnp.bfloat16)
    transit = (jax.nn.silu(project(normed, trans_gate)) * project(normed, trans_value)).astype(
        jnp.bfloat16
    )
    residual = residual + project(transit, trans_outproj)
    return residual.astype(jnp.bfloat16)


def solution(mesh):
    return jax.shard_map(
        on_device,
        mesh=mesh,
        in_specs=(
            P(("grp", "row"), "col", None),
            P(("grp", "row"), "col"),
            P("grp"),
            P(),
            P(),
            P(),
            P(),
            P(),
            P(),
            P(),
            P(),
            P(),
            P(),
        ),
        out_specs=P(("grp", "row", "col"), None, None),
        check_vma=False,
    )
```

profile of v0, /device:TPU:0, one launch (start us, length us, event | category | flops | bytes accessed | tf_op | source)
XLA Modules:
  0.0 74.4 jit_solution(2476864956810803245)
XLA Ops:
  0.0 1.3 %convert_element_type.110 = bf16[8,8]{1,0:T(8,128)(2,1)} convert(s32[8,8]{1,0:T(8,128)} %param.14) | non-fusion elementwise | flops 64 | bytes 384 | tf_op jit(solution)/shard_map/convert_element_type | solution.py:41
  1.3 4.2 %all-to-all-start.1 = ((bf16[4,2,8]{2,1,0:T(2,128)(2,1)}), bf16[4,2,8]{2,1,0:T(2,128)(2,1)S(1)}, u32[]{:S(2)}, u32[]{:S(2)}) async-start(bf16[4,2,8]{2,1,0:T(2,128)(2,1)} %bitcast.7), calls=%async_computation.1 | async-start | bytes 4096 | tf_op jit(solution)/shard_map/all_to_all | solution.py:40
  5.5 0.7 copy-done.10
  6.2 2.9 %all-to-all-done.1 = bf16[4,2,8]{2,1,0:T(2,128)(2,1)S(1)} async-done(((bf16[4,2,8]{2,1,0:T(2,128)(2,1)}), bf16[4,2,8]{2,1,0:T(2,128)(2,1)S(1)}, u32[]{:S(2)}, u32[]{:S(2)}) %all-to-all-start.1) | async-done | bytes 160 | tf_op jit(solution)/shard_map/all_to_all | solution.py:40
  9.2 3.3 %all-to-all-start = ((bf16[8,8,128]{2,1,0:T(8,128)(2,1)}), bf16[8,8,128]{2,1,0:T(8,128)(2,1)S(1)}, u32[]{:S(2)}, u32[]{:S(2)}) async-start(bf16[8,8,128]{2,1,0:T(8,128)(2,1)} %param.13), calls=%async_computation | async-start | bytes 32768 | tf_op jit(solution)/shard_map/all_to_all | solution.py:39
  12.5 0.1 reshape.162
  12.6 3.6 %all-to-all-done = bf16[8,8,128]{2,1,0:T(8,128)(2,1)S(1)} async-done(((bf16[8,8,128]{2,1,0:T(8,128)(2,1)}), bf16[8,8,128]{2,1,0:T(8,128)(2,1)S(1)}, u32[]{:S(2)}, u32[]{:S(2)}) %all-to-all-start) | async-done | bytes 16416 | tf_op jit(solution)/shard_map/all_to_all | solution.py:39
  16.3 0.1 bitcast_reduce_fusion
  16.4 0.2 fusion.50
  16.6 0.1 rsqrt.36
  16.7 0.2 fusion.8
  17.0 0.6 copy-done.6
  17.6 0.2 fusion.11
  17.8 0.1 copy.50
  17.9 0.8 %reshape.178 = bf16[4,2,2048]{2,1,0:T(2,128)(2,1)} reshape(bf16[128,2,2,32]{3,2,1,0:T(2,128)(2,1)S(1)} %bitcast.120) | data formatting | bytes 65536
  18.7 3.3 %all-to-all-start.2 = ((bf16[4,2,2048]{2,1,0:T(2,128)(2,1)}), bf16[4,2,2048]{2,1,0:T(2,128)(2,1)S(1)}, u32[]{:S(2)}, u32[]{:S(2)}) async-start(bf16[4,2,2048]{2,1,0:T(2,128)(2,1)} %reshape.178), calls=%async_computation.2 | async-start | bytes 65536 | tf_op jit(solution)/shard_map/all_to_all | solution.py:57
  22.0 3.9 %all-to-all-done.2 = bf16[4,2,2048]{2,1,0:T(2,128)(2,1)S(1)} async-done(((bf16[4,2,2048]{2,1,0:T(2,128)(2,1)}), bf16[4,2,2048]{2,1,0:T(2,128)(2,1)S(1)}, u32[]{:S(2)}, u32[]{:S(2)}) %all-to-all-start.2) | async-done | bytes 32800 | tf_op jit(solution)/shard_map/all_to_all | solution.py:57
  25.9 0.1 reshape.179
  26.0 0.1 copy.91
  26.1 0.1 fusion.65
  26.2 13.4 %all_gather.6 = bf16[32,32,32]{2,1,0:T(8,128)(2,1)S(1)} all-gather(bf16[32,8,32]{2,1,0:T(8,128)(2,1)S(1)} %bitcast.124), channel_id=1, replica_groups=mesh['grp'=2,'row'=4,'col'=4] {'row'}, dimensions={1}, use_global_device_ids=true | all-gather | bytes 81920 | tf_op jit(solution)/shard_map/all_gather | solution.py:62
  39.7 0.2 convolution_convert_fusion
  39.9 0.7 reshape.180
  40.7 3.4 %all-to-all-start.3 = ((bf16[4,2,1024]{2,1,0:T(2,128)(2,1)}), bf16[4,2,1024]{2,1,0:T(2,128)(2,1)S(1)}, u32[]{:S(2)}, u32[]{:S(2)}) async-start(bf16[4,2,1024]{2,1,0:T(2,128)(2,1)} %reshape.180), calls=%async_computation.3 | async-start | bytes 32768 | tf_op jit(solution)/shard_map/all_to_all | solution.py:66
  44.1 0.2 fusion.15
  44.3 3.6 %all-to-all-done.3 = bf16[4,2,1024]{2,1,0:T(2,128)(2,1)S(1)} async-done(((bf16[4,2,1024]{2,1,0:T(2,128)(2,1)}), bf16[4,2,1024]{2,1,0:T(2,128)(2,1)S(1)}, u32[]{:S(2)}, u32[]{:S(2)}) %all-to-all-start.3) | async-done | bytes 16416 | tf_op jit(solution)/shard_map/all_to_all | solution.py:66
  47.9 0.1 reshape.181
  48.1 0.1 copy.53
  48.2 0.1 reshape.163
  48.4 0.6 copy-done.2
  49.0 0.3 fusion.67
  49.3 0.2 multiply_reduce_fusion.2
  49.5 0.7 copy-done.9
  50.1 0.2 fusion.18
  50.3 19.4 %all_gather.7 = bf16[4,32,32]{2,0,1:T(4,128)(2,1)S(1)} all-gather(bf16[4,2,32]{2,0,1:T(4,128)(2,1)S(1)} %fusion.18), channel_id=1, replica_groups=mesh['grp'=2,'row'=4,'col'=4] {'row','col'}, dimensions={1}, use_global_device_ids=true | all-gather | bytes 8704 | tf_op jit(solution)/shard_map/all_gather | solution.py:93
  69.9 0.2 fusion.68
  70.1 0.1 reshape.158
  70.2 0.1 reshape.159
  70.3 0.1 copy.62
  70.5 0.2 fusion.69
  70.7 0.1 fusion.32
  70.9 0.7 copy-done.8
  71.6 0.2 fusion.70
  71.8 0.2 multiply_reduce_fusion.1
  72.0 0.5 copy-done.1
  72.5 0.2 fusion.22
  72.7 0.7 copy-done.3
  73.5 0.9 %fusion.17 = bf16[2,32,128]{2,1,0:T(8,128)(2,1)} fusion(f32[2,32,128]{2,1,0:T(8,128)S(1)} %get-tuple-element.16, bf16[512,128]{1,0:T(8,128)(2,1)S(1)} %copy-done.3, bf16[128,512]{1,0:T(8,128)(2,1)S(1)} %copy-done.4, f32[2,32,512]{2,1,0:T(8,128)S(1)} %fusion.22, f32[2,32]{1,0:T(2,128)S(1)} %add_rsqrt_fusion.1, f32[2,32]{1,0:T(2,128)S(1)} %broadcast_multiply_fusion.1), kind=kOutput, calls=%fused_computation.25 | convolution fusion | flops 17014784 | bytes 442880 | tf_op jit(solution)/shard_map/rkc,cd->rkd/dot_general | solution.py:18
  (41 shorter events, 0.7 us)
Async XLA Ops:
  0.0 69.9 %copy-start = (bf16[128,512]{1,0:T(8,128)(2,1)S(1)}, bf16[128,512]{1,0:T(8,128)(2,1)}, u32[]{:S(2)}) copy-start(bf16[128,512]{1,0:T(8,128)(2,1)} %param.20) | copy-start | bytes 393220
  1.3 7.9 %all-to-all-start.1 = ((bf16[4,2,8]{2,1,0:T(2,128)(2,1)}), bf16[4,2,8]{2,1,0:T(2,128)(2,1)S(1)}, u32[]{:S(2)}, u32[]{:S(2)}) async-start(bf16[4,2,8]{2,1,0:T(2,128)(2,1)} %bitcast.7), calls=%async_computation.1 | async-start | bytes 4096 | tf_op jit(solution)/shard_map/all_to_all | solution.py:40
  5.5 0.7 copy-start.10
  9.2 7.1 %all-to-all-start = ((bf16[8,8,128]{2,1,0:T(8,128)(2,1)}), bf16[8,8,128]{2,1,0:T(8,128)(2,1)S(1)}, u32[]{:S(2)}, u32[]{:S(2)}) async-start(bf16[8,8,128]{2,1,0:T(8,128)(2,1)} %param.13), calls=%async_computation | async-start | bytes 32768 | tf_op jit(solution)/shard_map/all_to_all | solution.py:39
  12.6 4.1 %copy-start.5 = (bf16[128,256]{1,0:T(8,128)(2,1)S(1)}, bf16[128,256]{1,0:T(8,128)(2,1)}, u32[]{:S(2)}) copy-start(bf16[128,256]{1,0:T(8,128)(2,1)} %param.16) | copy-start | bytes 196612
  16.7 0.9 %copy-start.6 = (bf16[128,256]{1,0:T(8,128)(2,1)S(1)}, bf16[128,256]{1,0:T(8,128)(2,1)}, u32[]{:S(2)}) copy-start(bf16[128,256]{1,0:T(8,128)(2,1)} %param.17) | copy-start | bytes 196612
  18.7 7.2 %all-to-all-start.2 = ((bf16[4,2,2048]{2,1,0:T(2,128)(2,1)}), bf16[4,2,2048]{2,1,0:T(2,128)(2,1)S(1)}, u32[]{:S(2)}, u32[]{:S(2)}) async-start(bf16[4,2,2048]{2,1,0:T(2,128)(2,1)} %reshape.178), calls=%async_computation.2 | async-start | bytes 65536 | tf_op jit(solution)/shard_map/all_to_all | solution.py:57
  40.7 3.4 %copy-start.7 = (bf16[128,128]{1,0:T(8,128)(2,1)S(1)}, bf16[128,128]{1,0:T(8,128)(2,1)}, u32[]{:S(2)}) copy-start(bf16[128,128]{1,0:T(8,128)(2,1)} %param.18) | copy-start | bytes 98308
  40.7 7.2 %all-to-all-start.3 = ((bf16[4,2,1024]{2,1,0:T(2,128)(2,1)}), bf16[4,2,1024]{2,1,0:T(2,128)(2,1)S(1)}, u32[]{:S(2)}, u32[]{:S(2)}) async-start(bf16[4,2,1024]{2,1,0:T(2,128)(2,1)} %reshape.180), calls=%async_computation.3 | async-start | bytes 32768 | tf_op jit(solution)/shard_map/all_to_all | solution.py:66
  48.2 0.8 %copy-start.2 = (bf16[128,128]{1,0:T(8,128)(2,1)S(1)}, bf16[128,128]{1,0:T(8,128)(2,1)}, u32[]{:S(2)}) copy-start(bf16[128,128]{1,0:T(8,128)(2,1)} %param.19) | copy-start | bytes 98308
  49.4 0.7 copy-start.9
  70.8 0.8 %copy-start.8 = (bf16[128,128]{1,0:T(8,128)(2,1)S(1)}, bf16[128,128]{1,0:T(8,128)(2,1)}, u32[]{:S(2)}) copy-start(bf16[128,128]{1,0:T(8,128)(2,1)} %param.22) | copy-start | bytes 98308
  71.6 0.9 %copy-start.1 = (bf16[128,512]{1,0:T(8,128)(2,1)S(1)}, bf16[128,512]{1,0:T(8,128)(2,1)}, u32[]{:S(2)}) copy-start(bf16[128,512]{1,0:T(8,128)(2,1)} %param.23) | copy-start | bytes 393220
  72.5 0.9 %copy-start.3 = (bf16[512,128]{1,0:T(8,128)(2,1)S(1)}, bf16[512,128]{1,0:T(8,128)(2,1)}, u32[]{:S(2)}) copy-start(bf16[512,128]{1,0:T(8,128)(2,1)} %param.25) | copy-start | bytes 393220
  72.5 1.0 %copy-start.4 = (bf16[128,512]{1,0:T(8,128)(2,1)S(1)}, bf16[128,512]{1,0:T(8,128)(2,1)}, u32[]{:S(2)}) copy-start(bf16[128,512]{1,0:T(8,128)(2,1)} %param.24) | copy-start | bytes 393220
where the time goes:
time: 75.1 us; the launch traced here: 74.4 us
  blocking collectives  32.9 us (44%)
  starting transfers between devices  14.1 us (19%)
  waiting for transfers between devices  14.1 us (19%)
  local copies, waits for them, and re-layouts  7.65 us (10%)
  matrix products  3.29 us (4%)
  other arithmetic  2.11 us (3%)
    all_gather x1, blocking collectives, on_device(): segment = lax.all_gather(bias_local, ('row', 'col'), axis=1, tiled=True)  19.4 us
    all_gather x1, blocking collectives, on_device(): lax.all_gather(spread_pair[1], 'row', axis=1, tiled=True)  13.4 us
    unnamed x26, local copies, waits for them, and re-layouts  6.29 us
    all_to_all x1, starting transfers between devices, on_device(): lax.all_to_all(pair_mask.astype(jnp.bfloat16), 'col', split_axis=0, conca...  4.21 us
    all_to_all x1, waiting for transfers between devices, on_device(): lax.all_to_all(paired, 'col', split_axis=1, concat_axis=2, tiled=True)  3.9 us
    all_to_all x1, waiting for transfers between devices, on_device(): lax.all_to_all(pair_track, 'col', split_axis=0, concat_axis=1, tiled=True)  3.64 us
    all_to_all x1, waiting for transfers between devices, on_device(): lax.all_to_all(crossed, 'col', split_axis=1, concat_axis=0, tiled=True)  3.59 us
    all_to_all x1, starting transfers between devices, on_device(): lax.all_to_all(crossed, 'col', split_axis=1, concat_axis=0, tiled=True)  3.39 us
  transfers between devices with their start and end apart: 4, of which 4 were waited for; matrix products, arithmetic and copies ran while one was open for 1% of the time, Pallas kernels for 0%

commit v1 on v0

--- a/solution.py
+++ b/solution.py
@@ -1,10 +1,264 @@
+import functools
+
 import jax
 import jax.numpy as jnp
 from jax import lax
+from jax.experimental import pallas as pl
+from jax.experimental.pallas import tpu as pltpu
 from jax.sharding import PartitionSpec as P
 
 epsilon = 1e-05
 masked_score = -1000000000.0
+crop_axes = ("row", "col")
+lanes = 128
+crop_bytes_max = 1 << 20
+
+
+def layer_norm(values):
+    center = values - jnp.mean(values, axis=-1, keepdims=True)
+    spread = jnp.mean(center * center, axis=-1, keepdims=True)
+    return center * lax.rsqrt(spread + epsilon)
+
+
+def sigmoid(values):
+    return 1.0 / (1.0 + jnp.exp(-values))
+
+
+def dot(left, right):
+    return jnp.dot(left, right, preferred_element_type=jnp.float32)
+
+
+def pack_kernel(track_ref, mask_ref, out_ref):
+    block_rows, block_cols = mask_ref.shape
+    pairs = block_rows * block_cols
+    width = out_ref.shape[1]
+    out_ref[:pairs, :] = track_ref[...]
+    below = out_ref.shape[0] - pairs
+    mask = mask_ref[...].astype(jnp.float32)
+    pick = (
+        lax.broadcasted_iota(jnp.int32, (below, block_cols), 0)
+        == lax.broadcasted_iota(jnp.int32, (below, block_cols), 1)
+    ).astype(jnp.float32)
+    place = (
+        lax.broadcasted_iota(jnp.int32, (block_rows, width), 0)
+        == lax.broadcasted_iota(jnp.int32, (block_rows, width), 1)
+    ).astype(jnp.float32)
+    turned = lax.dot_general(mask, place, (((0,), (0,)), ((), ())), preferred_element_type=jnp.float32)
+    out_ref[pairs:, :] = dot(pick, turned).astype(out_ref.dtype)
+
+
+def crop_kernel(
+    offsets,
+    col_count,
+    me_ref,
+    tokens_ref,
+    crop_ref,
+    token_col_ref,
+    mult_gate_ref,
+    mult_value_ref,
+    mult_outgate_ref,
+    mult_outproj_ref,
+    attn_proj_ref,
+    bias_wide_ref,
+    attn_outproj_ref,
+    trans_gate_ref,
+    trans_value_ref,
+    trans_outproj_ref,
+    out_ref,
+    track,
+    normed,
+    key_wide,
+    mult_wide,
+    left,
+    right,
+    outgate,
+    bias,
+):
+    length = tokens_ref.shape[0]
+    channels = track.shape[2]
+    hidden = mult_outproj_ref.shape[0]
+    own_rows = out_ref.shape[0] // length
+    inner = attn_outproj_ref.shape[0]
+    spans = bias_wide_ref.shape[1]
+    heads = spans // length
+    head_width = inner // heads
+    block_rows = length // (len(offsets) // col_count)
+    block_cols = length // col_count
+    pairs = block_rows * block_cols
+    me = me_ref[0]
+
+    token_col = token_col_ref[...]
+    for slot, offset in enumerate(offsets):
+        block = me ^ offset
+        first_row = (block // col_count) * block_rows
+        cols = pl.ds(pl.multiple_of((block % col_count) * block_cols, block_cols), block_cols)
+        values = crop_ref[slot, :pairs, :].astype(jnp.float32)
+        turned = crop_ref[slot, pairs:, :].astype(jnp.float32)[:block_cols]
+        rounded = layer_norm(values)
+        values = values.reshape(block_rows, block_cols, channels)
+        rounded = rounded.reshape(block_rows, block_cols, channels)
+        tokens = token_col_ref[cols, :]
+        for row in range(block_rows):
+            key = turned[:, row : row + 1] * tokens
+            track[first_row + row, cols, :] = values[row]
+            normed[first_row + row, cols, :] = rounded[row]
+            key_wide[first_row + row, cols, :] = key
+            mult_wide[first_row + row, cols, :] = key * tokens_ref[first_row + row].astype(jnp.float32)
+
+    step = block_rows
+    steps = length // step
+
+    @pl.loop(0, steps)
+    def _(index):
+        rows = pl.ds(index * step, step)
+        flat = pl.ds(pl.multiple_of(index * step * length, step * length), step * length)
+        source = normed[rows].reshape(step * length, channels).astype(jnp.bfloat16)
+        mask = mult_wide[rows].reshape(step * length, lanes)
+        paired = sigmoid(dot(source, mult_gate_ref[...])) * dot(source, mult_value_ref[...])
+        left[flat, :] = (paired[:, :hidden] * mask).astype(jnp.bfloat16).astype(jnp.float32)
+        right[flat, :] = (paired[:, hidden:] * mask).astype(jnp.bfloat16).astype(jnp.float32)
+        outgate[flat, :] = sigmoid(dot(source, mult_outgate_ref[...]))
+
+    head_of_lane = lax.broadcasted_iota(jnp.int32, (1, spans), 1) // length
+    key_of_lane = lax.broadcasted_iota(jnp.int32, (length, spans), 1) % length
+    on_key = (lax.broadcasted_iota(jnp.int32, (length, spans), 0) == key_of_lane).astype(jnp.float32)
+
+    def spread_keys(values):
+        values = values.reshape(values.shape[0] // length, length, spans)
+        return jnp.sum(values * on_key[None], axis=1)
+
+    @pl.loop(0, steps)
+    def _(index):
+        flat = pl.ds(pl.multiple_of(index * step * length, step * length), step * length)
+        total = [jnp.zeros((length, hidden), jnp.float32) for _ in range(step)]
+        for k in range(length):
+            column = right[pl.ds(k, length, stride=length), :]
+            for i in range(step):
+                total[i] = total[i] + left[pl.ds((index * step + i) * length + k, 1), :] * column
+        crossed = jnp.concatenate(total, axis=0).astype(jnp.bfloat16).astype(jnp.float32)
+        mixed = layer_norm(crossed).astype(jnp.bfloat16)
+        update = outgate[flat, :] * dot(mixed, mult_outproj_ref[...])
+        rows = pl.ds(index * step, step)
+        after = track[rows].reshape(step * length, channels) + update
+        again = layer_norm(after)
+        track[rows] = after.reshape(step, length, channels)
+        normed[rows] = again.reshape(step, length, channels)
+        wide = dot(again.astype(jnp.bfloat16), bias_wide_ref[...])
+        wide = wide.astype(jnp.bfloat16).astype(jnp.float32)
+        bias[rows, :] = spread_keys(wide)
+
+    own = pl.ds(me * own_rows, own_rows)
+    residual = track[own].reshape(own_rows * length, channels)
+    source = normed[own].reshape(own_rows * length, channels).astype(jnp.bfloat16)
+    projected = dot(source, attn_proj_ref[...])
+    queries = (projected[:, :inner] * head_width ** (-0.5)).astype(jnp.bfloat16)
+    keys = projected[:, inner : 2 * inner]
+    values = projected[:, 2 * inner : 3 * inner]
+    gating = sigmoid(projected[:, 3 * inner :])
+    allowed = spread_keys(key_wide[own].reshape(own_rows * length, spans)) > 0.5
+    head_of_row = lax.broadcasted_iota(jnp.int32, (spans, inner), 0) // length
+    head_of_channel = lax.broadcasted_iota(jnp.int32, (spans, inner), 1) // head_width
+    same_head = (head_of_row == head_of_channel).astype(jnp.float32)
+    gathered = []
+    for row in range(own_rows):
+        here = slice(row * length, (row + 1) * length)
+        tall_keys = (jnp.concatenate([keys[here]] * heads, axis=0) * same_head).astype(jnp.bfloat16)
+        tall_values = (jnp.concatenate([values[here]] * heads, axis=0) * same_head).astype(jnp.bfloat16)
+        scores = lax.dot_general(
+            queries[here], tall_keys, (((1,), (1,)), ((), ())), preferred_element_type=jnp.float32
+        )
+        scores = jnp.where(allowed[row : row + 1], scores + bias[...], masked_score)
+        top = jnp.zeros_like(scores)
+        for head in range(heads):
+            here_lanes = head_of_lane == head
+            most = jnp.max(jnp.where(here_lanes, scores, -jnp.inf), axis=1, keepdims=True)
+            top = jnp.where(here_lanes, most, top)
+        expo = jnp.exp(scores - top)
+        whole = jnp.zeros_like(scores)
+        for head in range(heads):
+            here_lanes = head_of_lane == head
+            part = jnp.sum(jnp.where(here_lanes, expo, 0.0), axis=1, keepdims=True)
+            whole = jnp.where(here_lanes, part, whole)
+        gathered.append(dot((expo / whole).astype(jnp.bfloat16), tall_values))
+    gated = (gating * jnp.concatenate(gathered, axis=0)).astype(jnp.bfloat16)
+    residual = residual + dot(gated, attn_outproj_ref[...])
+    source = layer_norm(residual).astype(jnp.bfloat16)
+    gate = dot(source, trans_gate_ref[...])
+    transit = (gate * sigmoid(gate) * dot(source, trans_value_ref[...])).astype(jnp.bfloat16)
+    out_ref[...] = (residual + dot(transit, trans_outproj_ref[...])).astype(out_ref.dtype)
+
+
+def gathered_crop(
+    pair_track,
+    pair_mask,
+    token_mask,
+    mult_gate,
+    mult_value,
+    mult_outgate,
+    mult_outproj,
+    attn_proj,
+    attn_bias,
+    attn_outproj,
+    trans_gate,
+    trans_value,
+    trans_outproj,
+):
+    row_count, col_count = lax.axis_size("row"), lax.axis_size("col")
+    devices = row_count * col_count
+    block_rows, block_cols, channels = pair_track.shape
+    length = block_cols * col_count
+    pairs = block_rows * block_cols
+    own_rows = length // devices
+    me = lax.axis_index(crop_axes)
+    in_vmem = pl.BlockSpec(memory_space=pltpu.VMEM)
+    in_smem = pl.BlockSpec(memory_space=pltpu.SMEM)
+    block = pl.pallas_call(
+        pack_kernel,
+        out_shape=jax.ShapeDtypeStruct((pairs + 16, channels), pair_track.dtype),
+        in_specs=[in_vmem, in_vmem],
+        out_specs=in_vmem,
+        name="pack",
+    )(pair_track.reshape(pairs, channels), pair_mask)
+    crop = block[None]
+    offsets = [0]
+    mask = devices // 2
+    while mask:
+        turn = mask | 1
+        crop = jnp.concatenate(
+            [crop, lax.ppermute(crop, crop_axes, [(i, i ^ turn) for i in range(devices)])]
+        )
+        offsets = offsets + [offset ^ turn for offset in offsets]
+        mask //= 2
+    heads = attn_bias.shape[1]
+    token_col = jnp.broadcast_to(token_mask.astype(jnp.float32)[:, None], (length, lanes))
+    bias_wide = jnp.repeat(attn_bias, length, axis=1)
+    whole = pltpu.VMEM((length, length, channels), jnp.float32)
+    flat = pltpu.VMEM((length * length, channels), jnp.float32)
+    out = pl.pallas_call(
+        functools.partial(crop_kernel, tuple(offsets), col_count),
+        out_shape=jax.ShapeDtypeStruct((own_rows * length, channels), jnp.bfloat16),
+        in_specs=[in_smem, in_smem] + [in_vmem] * 12,
+        out_specs=in_vmem,
+        scratch_shapes=[whole, whole, whole, whole, flat, flat, flat, pltpu.VMEM((length, heads * length), jnp.float32)],
+        compiler_params=pltpu.CompilerParams(vmem_limit_bytes=48 << 20),
+        name="crop",
+    )(
+        me.astype(jnp.int32)[None],
+        token_mask,
+        crop,
+        token_col,
+        mult_gate,
+        mult_value,
+        mult_outgate,
+        mult_outproj,
+        attn_proj,
+        bias_wide,
+        attn_outproj,
+        trans_gate,
+        trans_value,
+        trans_outproj,
+    )
+    return out.reshape(own_rows, length, channels)
 
 
 def normalize(values, axis):
@@ -18,7 +272,7 @@
     return jnp.einsum("rkc,cd->rkd", normed, weight, preferred_element_type=jnp.float32)
 
 
-def on_device(
+def split_crop(
     pair_track,
     pair_mask,
     token_mask,
@@ -114,6 +368,17 @@
     return residual.astype(jnp.bfloat16)
 
 
+def on_device(pair_track, *others):
+    devices = lax.axis_size("row") * lax.axis_size("col")
+    pairs = pair_track.shape[0] * pair_track.shape[1] * devices
+    heads = others[7].shape[1]
+    length = pair_track.shape[1] * lax.axis_size("col")
+    fits = pairs * pair_track.shape[2] * 4 <= crop_bytes_max
+    if fits and heads * length == lanes and pair_track.shape[2] == lanes and devices & (devices - 1) == 0:
+        return gathered_crop(pair_track, *others)
+    return split_crop(pair_track, *others)
+
+
 def solution(mesh):
     return jax.shard_map(
         on_device,

time: 75.1 us -> 27.6 us (0.37)
  blocking collectives: 32.9 us -> 0 us
  Pallas kernels: 0 us -> 11.6 us
  waiting for transfers between devices: 14.1 us -> 5.48 us
  starting transfers between devices: 14.1 us -> 7.55 us
  local copies, waits for them, and re-layouts: 7.65 us -> 1.63 us
  matrix products: 3.29 us -> 0 us
  other arithmetic: 2.11 us -> 0.77 us
    all_gather x2 -> x0, blocking collectives: 32.9 us -> none  [the longest x1 19.4 us: on_device(): segment = lax.all_gather(bias_local, ('row', 'col'), axis=1, tiled=True)]
    all_to_all x4 -> x0, starting transfers between devices: 14.1 us -> none  [the longest x1 4.21 us: on_device(): lax.all_to_all(pair_mask.astype(jnp.bfloat16), 'col', split_axis=0, conca...]
    all_to_all x4 -> x0, waiting for transfers between devices: 14.1 us -> none  [the longest x1 3.9 us: on_device(): lax.all_to_all(paired, 'col', split_axis=1, concat_axis=2, tiled=True)]
    pallas_call x0 -> x2, Pallas kernels: none -> 11.6 us  [the longest x1 9.99 us: gathered_crop(): pl.pallas_call(functools.partial(crop_kernel, tuple(offsets), col_count),...]
    ppermute x0 -> x4, starting transfers between devices: none -> 7.55 us  [gathered_crop(): lax.ppermute(crop, crop_axes, [(i, i ^ turn) for i in range(devices)])]
    ppermute x0 -> x4, waiting for transfers between devices: none -> 5.48 us  [gathered_crop(): lax.ppermute(crop, crop_axes, [(i, i ^ turn) for i in range(devices)])]
    unnamed x26 -> x28, local copies, waits for them, and re-layouts: 6.29 us -> 1.41 us
    dot_general x11 -> x0, matrix products: 3.07 us -> none  [the longest x4 1.57 us: project(): jnp.einsum('rkc,cd->rkd', normed, weight, preferred_element_type=jnp.floa...]
where the time goes in v1:
time: 27.6 us; the launch traced here: 27.2 us
  Pallas kernels  11.6 us (42%)
  starting transfers between devices  7.55 us (27%)
  waiting for transfers between devices  5.48 us (20%)
  local copies, waits for them, and re-layouts  1.63 us (6%)
  other arithmetic  0.77 us (3%)
    pallas_call x1, Pallas kernels, gathered_crop(): pl.pallas_call(functools.partial(crop_kernel, tuple(offsets), col_count),...  9.99 us
    ppermute x4, starting transfers between devices, gathered_crop(): lax.ppermute(crop, crop_axes, [(i, i ^ turn) for i in range(devices)])  7.55 us
    ppermute x4, waiting for transfers between devices, gathered_crop(): lax.ppermute(crop, crop_axes, [(i, i ^ turn) for i in range(devices)])  5.48 us
    pallas_call x1, Pallas kernels, gathered_crop(): pl.pallas_call(pack_kernel, out_shape=jax.ShapeDtypeStruct((pairs + 16, c...  1.61 us
    unnamed x28, local copies, waits for them, and re-layouts  1.41 us
    concatenate x3, other arithmetic, gathered_crop(): jnp.concatenate([crop, lax.ppermute(crop, crop_axes, [(i, i ^ turn) for i...  0.76 us
  transfers between devices with their start and end apart: 4, of which 4 were waited for; matrix products, arithmetic and copies ran while one was open for 1% of the time, Pallas kernels for 0%

profile of v1, /device:TPU:0, one launch (start us, length us, event | category | flops | bytes accessed | tf_op | source)
XLA Modules:
  0.0 27.2 jit_solution(9443527876077696007)
XLA Ops:
  0.0 1.6 %pack.1 = bf16[80,128]{1,0:T(8,128)(2,1)} custom-call(bf16[64,128]{1,0:T(8,128)(2,1)} %bitcast.11, s32[8,8]{1,0:T(8,128)} %mask_ref.1), custom_call_target="tpu_custom_call" | custom-call | tf_op jit(solution)/shard_map/pack/pallas_call | solution.py:215
  1.6 0.0 copy-start.10
  1.6 3.5 %collective-permute-start = (bf16[1,80,128]{2,1,0:T(8,128)(2,1)}, bf16[1,80,128]{2,1,0:T(8,128)(2,1)S(1)}, u32[]{:S(2)}, u32[]{:S(2)}) collective-permute-start(bf16[1,80,128]{2,1,0:T(8,128)(2,1)} %bitcast.6), channel_id=1, source_target_pairs={{0,9},{1,8},{2,11},{3,10},{4,13},{5,12},{6,15},{7,14},{8,1},{9,0},... | collective-permute-start | bytes 61448 | tf_op jit(solution)/shard_map/ppermute | solution.py:228
  5.1 1.7 %collective-permute-done = bf16[1,80,128]{2,1,0:T(8,128)(2,1)S(1)} collective-permute-done((bf16[1,80,128]{2,1,0:T(8,128)(2,1)}, bf16[1,80,128]{2,1,0:T(8,128)(2,1)S(1)}, u32[]{:S(2)}, u32[]{:S(2)}) %collective-permute-start) | collective-permute-done | bytes 20512 | tf_op jit(solution)/shard_map/ppermute | solution.py:228
  6.8 0.7 %pad_maximum_fusion.2 = bf16[2,80,128]{2,1,0:T(8,128)(2,1)S(1)} fusion(bf16[1,80,128]{2,1,0:T(8,128)(2,1)S(1)} %collective-permute-done, bf16[1,80,128]{2,1,0:T(8,128)(2,1)} %bitcast.7), kind=kLoop, calls=%fused_computation.2 | loop fusion | flops 20480 | bytes 81920 | tf_op jit(solution)/shard_map/concatenate | solution.py:227
  7.6 1.9 %collective-permute-start.1 = (bf16[2,80,128]{2,1,0:T(8,128)(2,1)S(1)}, bf16[2,80,128]{2,1,0:T(8,128)(2,1)S(1)}, u32[]{:S(2)}, u32[]{:S(2)}) collective-permute-start(bf16[2,80,128]{2,1,0:T(8,128)(2,1)S(1)} %pad_maximum_fusion.2), channel_id=1, source_target_pairs={{0,5},{1,4},{2,7},{3,6},{4,1},{5,0},{6,3},{7,2},{8,13},{9,12},{10,... | collective-permute-start | bytes 122888 | tf_op jit(solution)/shard_map/ppermute | solution.py:228
  9.4 0.0 copy-done.10
  9.4 0.0 copy-start.9
  9.4 0.7 %copy-done.9 = s32[32]{0:T(128)S(1)} copy-done((s32[32]{0:T(128)S(1)}, s32[32]{0:T(128)}, u32[]{:S(2)}) %copy-start.9) | copy-done | bytes 152
  10.1 0.0 copy-start.11
  10.1 0.7 %copy-done.11 = bf16[128,4]{0,1:T(4,128)(2,1)S(1)} copy-done((bf16[128,4]{0,1:T(4,128)(2,1)S(1)}, bf16[128,4]{0,1:T(4,128)(2,1)}, u32[]{:S(2)}) %copy-start.11) | copy-done | bytes 1048
  10.8 0.1 copy.15.bias_wide_ref
  10.9 0.2 collective-permute-done.1
  11.1 1.8 %collective-permute-start.2 = (bf16[4,80,128]{2,1,0:T(8,128)(2,1)S(1)}, bf16[4,80,128]{2,1,0:T(8,128)(2,1)S(1)}, u32[]{:S(2)}, u32[]{:S(2)}) collective-permute-start(bf16[4,80,128]{2,1,0:T(8,128)(2,1)S(1)} %pad_maximum_fusion.1), channel_id=1, source_target_pairs={{0,3},{1,2},{2,1},{3,0},{4,7},{5,6},{6,5},{7,4},{8,11},{9,10},{10,... | collective-permute-start | bytes 245768 | tf_op jit(solution)/shard_map/ppermute | solution.py:228
  13.0 2.5 %collective-permute-done.2 = bf16[4,80,128]{2,1,0:T(8,128)(2,1)S(1)} collective-permute-done((bf16[4,80,128]{2,1,0:T(8,128)(2,1)S(1)}, bf16[4,80,128]{2,1,0:T(8,128)(2,1)S(1)}, u32[]{:S(2)}, u32[]{:S(2)}) %collective-permute-start.2) | collective-permute-done | bytes 81952 | tf_op jit(solution)/shard_map/ppermute | solution.py:228
  15.5 0.0 copy-start.5
  15.5 0.0 copy-start.6
  15.5 0.0 copy-start.7
  15.5 0.0 copy-start.8
  15.5 0.4 %collective-permute-start.3 = (bf16[8,80,128]{2,1,0:T(8,128)(2,1)S(1)}, bf16[8,80,128]{2,1,0:T(8,128)(2,1)S(1)}, u32[]{:S(2)}, u32[]{:S(2)}) collective-permute-start(bf16[8,80,128]{2,1,0:T(8,128)(2,1)S(1)} %pad_maximum_fusion), channel_id=1, source_target_pairs={{0,1},{1,0},{2,3},{3,2},{4,5},{5,4},{6,7},{7,6},{8,9},{9,8},{10,11... | collective-permute-start | bytes 491528 | tf_op jit(solution)/shard_map/ppermute | solution.py:228
  15.9 0.0 copy-start.3
  15.9 0.0 copy-start.2
  16.0 0.0 copy-start
  16.0 0.0 copy-start.1
  16.0 0.0 copy-start.4
  16.0 1.0 %collective-permute-done.3 = bf16[8,80,128]{2,1,0:T(8,128)(2,1)S(1)} collective-permute-done((bf16[8,80,128]{2,1,0:T(8,128)(2,1)S(1)}, bf16[8,80,128]{2,1,0:T(8,128)(2,1)S(1)}, u32[]{:S(2)}, u32[]{:S(2)}) %collective-permute-start.3) | collective-permute-done | bytes 163872 | tf_op jit(solution)/shard_map/ppermute | solution.py:228
  17.0 0.1 broadcast_in_dim.17.token_col_ref
  17.1 0.0 copy-done.5
  17.1 0.0 copy-done.6
  17.1 0.0 copy-done.7
  17.1 0.0 copy-done.8
  17.1 0.0 copy-done.3
  17.1 0.0 copy-done.2
  17.1 0.0 copy-done
  17.1 0.0 copy-done.1
  17.2 0.0 copy-done.4
  17.2 10.0 %crop.1 = bf16[64,128]{1,0:T(8,128)(2,1)} custom-call(s32[1]{0:T(128)} %bitcast.me_ref, s32[32]{0:T(128)S(1)} %copy-done.9, bf16[16,80,128]{2,1,0:T(8,128)(2,1)S(1)} %constant_dynamic-update-slice_fusion.crop_ref, f32[32,128]{1,0:T(8,128)S(1)} %broadcast_in_dim.17.token_col_ref, bf16[128,256]{1,0:T(8,128)(2,1)S(1)} %copy-done.4, ...), custom_call_target="tpu_custom_call" | custom-call | tf_op jit(solution)/shard_map/crop/pallas_call | solution.py:237
  (9 shorter events, 0.1 us)
Async XLA Ops:
  1.6 7.8 %copy-start.10 = (bf16[80,128]{1,0:T(8,128)(2,1)S(1)}, bf16[80,128]{1,0:T(8,128)(2,1)}, u32[]{:S(2)}) copy-start(bf16[80,128]{1,0:T(8,128)(2,1)} %pack.1) | copy-start | bytes 61444
  1.6 5.2 %collective-permute-start = (bf16[1,80,128]{2,1,0:T(8,128)(2,1)}, bf16[1,80,128]{2,1,0:T(8,128)(2,1)S(1)}, u32[]{:S(2)}, u32[]{:S(2)}) collective-permute-start(bf16[1,80,128]{2,1,0:T(8,128)(2,1)} %bitcast.6), channel_id=1, source_target_pairs={{0,9},{1,8},{2,11},{3,10},{4,13},{5,12},{6,15},{7,14},{8,1},{9,0},... | collective-permute-start | bytes 61448 | tf_op jit(solution)/shard_map/ppermute | solution.py:228
  7.6 3.5 %collective-permute-start.1 = (bf16[2,80,128]{2,1,0:T(8,128)(2,1)S(1)}, bf16[2,80,128]{2,1,0:T(8,128)(2,1)S(1)}, u32[]{:S(2)}, u32[]{:S(2)}) collective-permute-start(bf16[2,80,128]{2,1,0:T(8,128)(2,1)S(1)} %pad_maximum_fusion.2), channel_id=1, source_target_pairs={{0,5},{1,4},{2,7},{3,6},{4,1},{5,0},{6,3},{7,2},{8,13},{9,12},{10,... | collective-permute-start | bytes 122888 | tf_op jit(solution)/shard_map/ppermute | solution.py:228
  9.4 0.7 %copy-start.9 = (s32[32]{0:T(128)S(1)}, s32[32]{0:T(128)}, u32[]{:S(2)}) copy-start(s32[32]{0:T(128)} %tokens_ref.1) | copy-start | bytes 388
  10.1 0.7 %copy-start.11 = (bf16[128,4]{0,1:T(4,128)(2,1)S(1)}, bf16[128,4]{0,1:T(4,128)(2,1)}, u32[]{:S(2)}) copy-start(bf16[128,4]{0,1:T(4,128)(2,1)} %param.21) | copy-start | bytes 3076
  11.1 4.4 %collective-permute-start.2 = (bf16[4,80,128]{2,1,0:T(8,128)(2,1)S(1)}, bf16[4,80,128]{2,1,0:T(8,128)(2,1)S(1)}, u32[]{:S(2)}, u32[]{:S(2)}) collective-permute-start(bf16[4,80,128]{2,1,0:T(8,128)(2,1)S(1)} %pad_maximum_fusion.1), channel_id=1, source_target_pairs={{0,3},{1,2},{2,1},{3,0},{4,7},{5,6},{6,5},{7,4},{8,11},{9,10},{10,... | collective-permute-start | bytes 245768 | tf_op jit(solution)/shard_map/ppermute | solution.py:228
  15.5 1.6 %copy-start.5 = (bf16[128,256]{1,0:T(8,128)(2,1)S(1)}, bf16[128,256]{1,0:T(8,128)(2,1)}, u32[]{:S(2)}) copy-start(bf16[128,256]{1,0:T(8,128)(2,1)} %mult_value_ref.1) | copy-start | bytes 196612
  15.5 1.6 %copy-start.6 = (bf16[128,128]{1,0:T(8,128)(2,1)S(1)}, bf16[128,128]{1,0:T(8,128)(2,1)}, u32[]{:S(2)}) copy-start(bf16[128,128]{1,0:T(8,128)(2,1)} %mult_outgate_ref.1) | copy-start | bytes 98308
  15.5 1.6 %copy-start.7 = (bf16[128,128]{1,0:T(8,128)(2,1)S(1)}, bf16[128,128]{1,0:T(8,128)(2,1)}, u32[]{:S(2)}) copy-start(bf16[128,128]{1,0:T(8,128)(2,1)} %mult_outproj_ref.1) | copy-start | bytes 98308
  15.5 1.6 %copy-start.8 = (bf16[128,128]{1,0:T(8,128)(2,1)S(1)}, bf16[128,128]{1,0:T(8,128)(2,1)}, u32[]{:S(2)}) copy-start(bf16[128,128]{1,0:T(8,128)(2,1)} %attn_outproj_ref.1) | copy-start | bytes 98308
  15.5 1.5 %collective-permute-start.3 = (bf16[8,80,128]{2,1,0:T(8,128)(2,1)S(1)}, bf16[8,80,128]{2,1,0:T(8,128)(2,1)S(1)}, u32[]{:S(2)}, u32[]{:S(2)}) collective-permute-start(bf16[8,80,128]{2,1,0:T(8,128)(2,1)S(1)} %pad_maximum_fusion), channel_id=1, source_target_pairs={{0,1},{1,0},{2,3},{3,2},{4,5},{5,4},{6,7},{7,6},{8,9},{9,8},{10,11... | collective-permute-start | bytes 491528 | tf_op jit(solution)/shard_map/ppermute | solution.py:228
  15.9 1.2 %copy-start.3 = (bf16[512,128]{1,0:T(8,128)(2,1)S(1)}, bf16[512,128]{1,0:T(8,128)(2,1)}, u32[]{:S(2)}) copy-start(bf16[512,128]{1,0:T(8,128)(2,1)} %trans_outproj_ref.1) | copy-start | bytes 393220
  15.9 1.2 %copy-start.2 = (bf16[128,512]{1,0:T(8,128)(2,1)S(1)}, bf16[128,512]{1,0:T(8,128)(2,1)}, u32[]{:S(2)}) copy-start(bf16[128,512]{1,0:T(8,128)(2,1)} %trans_value_ref.1) | copy-start | bytes 393220
  16.0 1.2 %copy-start = (bf16[128,512]{1,0:T(8,128)(2,1)S(1)}, bf16[128,512]{1,0:T(8,128)(2,1)}, u32[]{:S(2)}) copy-start(bf16[128,512]{1,0:T(8,128)(2,1)} %attn_proj_ref.1) | copy-start | bytes 393220
  16.0 1.2 %copy-start.1 = (bf16[128,512]{1,0:T(8,128)(2,1)S(1)}, bf16[128,512]{1,0:T(8,128)(2,1)}, u32[]{:S(2)}) copy-start(bf16[128,512]{1,0:T(8,128)(2,1)} %trans_gate_ref.1) | copy-start | bytes 393220
  16.0 1.2 %copy-start.4 = (bf16[128,256]{1,0:T(8,128)(2,1)S(1)}, bf16[128,256]{1,0:T(8,128)(2,1)}, u32[]{:S(2)}) copy-start(bf16[128,256]{1,0:T(8,128)(2,1)} %mult_gate_ref.1) | copy-start | bytes 196612

commit v2 on v1

--- a/solution.py
+++ b/solution.py
@@ -14,46 +14,37 @@
 crop_bytes_max = 1 << 20
 
 
+def dot(left, right):
+    return jnp.dot(left, right, preferred_element_type=jnp.float32)
+
+
+def sigmoid(values):
+    return 1.0 / (1.0 + jnp.exp(-values))
+
+
 def layer_norm(values):
     center = values - jnp.mean(values, axis=-1, keepdims=True)
     spread = jnp.mean(center * center, axis=-1, keepdims=True)
     return center * lax.rsqrt(spread + epsilon)
 
 
-def sigmoid(values):
-    return 1.0 / (1.0 + jnp.exp(-values))
-
-
-def dot(left, right):
-    return jnp.dot(left, right, preferred_element_type=jnp.float32)
-
-
-def pack_kernel(track_ref, mask_ref, out_ref):
-    block_rows, block_cols = mask_ref.shape
-    pairs = block_rows * block_cols
-    width = out_ref.shape[1]
-    out_ref[:pairs, :] = track_ref[...]
-    below = out_ref.shape[0] - pairs
-    mask = mask_ref[...].astype(jnp.float32)
-    pick = (
-        lax.broadcasted_iota(jnp.int32, (below, block_cols), 0)
-        == lax.broadcasted_iota(jnp.int32, (below, block_cols), 1)
-    ).astype(jnp.float32)
-    place = (
-        lax.broadcasted_iota(jnp.int32, (block_rows, width), 0)
-        == lax.broadcasted_iota(jnp.int32, (block_rows, width), 1)
-    ).astype(jnp.float32)
-    turned = lax.dot_general(mask, place, (((0,), (0,)), ((), ())), preferred_element_type=jnp.float32)
-    out_ref[pairs:, :] = dot(pick, turned).astype(out_ref.dtype)
+def slot_index(offset, devices):
+    top = devices.bit_length() - 2
+    slot = offset & 1
+    for bit in range(1, top + 1):
+        slot = slot ^ ((offset >> bit) & 1)
+    slot = slot << top
+    for bit in range(1, top + 1):
+        slot = slot | (((offset >> bit) & 1) << (top - bit))
+    return slot
 
 
 def crop_kernel(
-    offsets,
+    slots,
     col_count,
-    me_ref,
-    tokens_ref,
     crop_ref,
-    token_col_ref,
+    token_pair_ref,
+    key_place_ref,
     mult_gate_ref,
     mult_value_ref,
     mult_outgate_ref,
@@ -65,97 +56,111 @@
     trans_value_ref,
     trans_outproj_ref,
     out_ref,
-    track,
-    normed,
-    key_wide,
-    mult_wide,
     left,
     right,
     outgate,
+    product,
+    after,
     bias,
+    key_lane,
 ):
-    length = tokens_ref.shape[0]
-    channels = track.shape[2]
+    channels = after.shape[1]
     hidden = mult_outproj_ref.shape[0]
-    own_rows = out_ref.shape[0] // length
     inner = attn_outproj_ref.shape[0]
-    spans = bias_wide_ref.shape[1]
+    length, spans = bias.shape
     heads = spans // length
     head_width = inner // heads
-    block_rows = length // (len(offsets) // col_count)
-    block_cols = length // col_count
+    own_rows = out_ref.shape[0] // length
+    devices = len(slots)
+    row_count = devices // col_count
+    block_rows, block_cols = length // row_count, length // col_count
     pairs = block_rows * block_cols
-    me = me_ref[0]
-
-    token_col = token_col_ref[...]
-    for slot, offset in enumerate(offsets):
-        block = me ^ offset
-        first_row = (block // col_count) * block_rows
-        cols = pl.ds(pl.multiple_of((block % col_count) * block_cols, block_cols), block_cols)
-        values = crop_ref[slot, :pairs, :].astype(jnp.float32)
-        turned = crop_ref[slot, pairs:, :].astype(jnp.float32)[:block_cols]
-        rounded = layer_norm(values)
-        values = values.reshape(block_rows, block_cols, channels)
-        rounded = rounded.reshape(block_rows, block_cols, channels)
-        tokens = token_col_ref[cols, :]
+    whole = length * length
+    me = lax.axis_index(crop_axes)
+
+    def slot_at(row, col):
+        return slot_index((row * col_count + col) ^ me, devices)
+
+    packed = crop_ref[:, :pairs, :].reshape(whole, channels)
+    source = layer_norm(packed.astype(jnp.float32)).astype(jnp.bfloat16)
+    diagonal = (
+        lax.broadcasted_iota(jnp.int32, (block_cols, lanes), 0)
+        == lax.broadcasted_iota(jnp.int32, (block_cols, lanes), 1)
+    ).astype(jnp.float32)
+    masks = []
+    for slot, offset in enumerate(slots):
+        mask = crop_ref[slot, pairs:, :].astype(jnp.float32)[:block_rows] * token_pair_ref[me ^ offset]
+        masks.append((mask[:, None, :] * diagonal[None]).reshape(pairs, lanes))
+    mask = dot(jnp.concatenate(masks, axis=0).astype(jnp.bfloat16), jnp.ones((lanes, channels), jnp.bfloat16))
+    outgate[...] = sigmoid(dot(source, mult_outgate_ref[...]))
+    paired = sigmoid(dot(source, mult_gate_ref[...])) * dot(source, mult_value_ref[...])
+    left[...] = (paired[:, :hidden] * mask).astype(jnp.bfloat16).astype(jnp.float32)
+    turned = (paired[:, hidden:] * mask).astype(jnp.bfloat16).astype(jnp.float32)
+    for slot in range(devices):
         for row in range(block_rows):
-            key = turned[:, row : row + 1] * tokens
-            track[first_row + row, cols, :] = values[row]
-            normed[first_row + row, cols, :] = rounded[row]
-            key_wide[first_row + row, cols, :] = key
-            mult_wide[first_row + row, cols, :] = key * tokens_ref[first_row + row].astype(jnp.float32)
-
-    step = block_rows
-    steps = length // step
-
-    @pl.loop(0, steps)
-    def _(index):
-        rows = pl.ds(index * step, step)
-        flat = pl.ds(pl.multiple_of(index * step * length, step * length), step * length)
-        source = normed[rows].reshape(step * length, channels).astype(jnp.bfloat16)
-        mask = mult_wide[rows].reshape(step * length, lanes)
-        paired = sigmoid(dot(source, mult_gate_ref[...])) * dot(source, mult_value_ref[...])
-        left[flat, :] = (paired[:, :hidden] * mask).astype(jnp.bfloat16).astype(jnp.float32)
-        right[flat, :] = (paired[:, hidden:] * mask).astype(jnp.bfloat16).astype(jnp.float32)
-        outgate[flat, :] = sigmoid(dot(source, mult_outgate_ref[...]))
-
-    head_of_lane = lax.broadcasted_iota(jnp.int32, (1, spans), 1) // length
+            start = slot * pairs + row * block_cols
+            right[pl.ds(slot * pairs + row, block_cols, stride=block_rows), :] = turned[start : start + block_cols]
+
+    starts = [[slot_at(row, col) * pairs for col in range(col_count)] for row in range(row_count)]
+
+    @pl.loop(0, row_count)
+    def _(part):
+        total = [jnp.zeros((length, hidden), jnp.float32) for _ in range(block_rows)]
+        for col in range(col_count):
+            start = slot_at(part, col) * pairs
+            for k in range(block_cols):
+                column = jnp.concatenate(
+                    [
+                        right[pl.ds(pl.multiple_of(starts[row][col] + k * block_rows, block_rows), block_rows), :]
+                        for row in range(row_count)
+                    ],
+                    axis=0,
+                )
+                for row in range(block_rows):
+                    total[row] = total[row] + left[pl.ds(start + row * block_cols + k, 1), :] * column
+        step = block_rows * length
+        product[pl.ds(pl.multiple_of(part * step, step), step), :] = jnp.concatenate(total, axis=0)
+
+    def absolute(load):
+        return jnp.concatenate(
+            [
+                jnp.concatenate(
+                    [load(row, col).reshape(block_rows, block_cols, channels) for col in range(col_count)], axis=1
+                )
+                for row in range(row_count)
+            ],
+            axis=0,
+        ).reshape(whole, channels)
+
+    crossed = product[...].astype(jnp.bfloat16).astype(jnp.float32)
+    mixed = layer_norm(crossed).astype(jnp.bfloat16)
+    gate = absolute(lambda row, col: outgate[pl.ds(pl.multiple_of(starts[row][col], pairs), pairs), :])
+    track = absolute(lambda row, col: crop_ref[slot_at(row, col), :pairs, :].astype(jnp.float32))
+    summed = track + gate * dot(mixed, mult_outproj_ref[...])
+    after[...] = summed
+    again = layer_norm(summed)
+    product[...] = again
     key_of_lane = lax.broadcasted_iota(jnp.int32, (length, spans), 1) % length
     on_key = (lax.broadcasted_iota(jnp.int32, (length, spans), 0) == key_of_lane).astype(jnp.float32)
-
-    def spread_keys(values):
-        values = values.reshape(values.shape[0] // length, length, spans)
-        return jnp.sum(values * on_key[None], axis=1)
-
-    @pl.loop(0, steps)
-    def _(index):
-        flat = pl.ds(pl.multiple_of(index * step * length, step * length), step * length)
-        total = [jnp.zeros((length, hidden), jnp.float32) for _ in range(step)]
-        for k in range(length):
-            column = right[pl.ds(k, length, stride=length), :]
-            for i in range(step):
-                total[i] = total[i] + left[pl.ds((index * step + i) * length + k, 1), :] * column
-        crossed = jnp.concatenate(total, axis=0).astype(jnp.bfloat16).astype(jnp.float32)
-        mixed = layer_norm(crossed).astype(jnp.bfloat16)
-        update = outgate[flat, :] * dot(mixed, mult_outproj_ref[...])
-        rows = pl.ds(index * step, step)
-        after = track[rows].reshape(step * length, channels) + update
-        again = layer_norm(after)
-        track[rows] = after.reshape(step, length, channels)
-        normed[rows] = again.reshape(step, length, channels)
-        wide = dot(again.astype(jnp.bfloat16), bias_wide_ref[...])
-        wide = wide.astype(jnp.bfloat16).astype(jnp.float32)
-        bias[rows, :] = spread_keys(wide)
-
-    own = pl.ds(me * own_rows, own_rows)
-    residual = track[own].reshape(own_rows * length, channels)
-    source = normed[own].reshape(own_rows * length, channels).astype(jnp.bfloat16)
+    wide = dot(again.astype(jnp.bfloat16), bias_wide_ref[...]).astype(jnp.bfloat16).astype(jnp.float32)
+    bias[...] = jnp.sum(wide.reshape(length, length, spans) * on_key[None], axis=1)
+
+    own = pl.ds(pl.multiple_of(me * own_rows * length, own_rows * length), own_rows * length)
+    residual = after[own, :]
+    source = product[own, :].astype(jnp.bfloat16)
     projected = dot(source, attn_proj_ref[...])
     queries = (projected[:, :inner] * head_width ** (-0.5)).astype(jnp.bfloat16)
     keys = projected[:, inner : 2 * inner]
     values = projected[:, 2 * inner : 3 * inner]
     gating = sigmoid(projected[:, 3 * inner :])
-    allowed = spread_keys(key_wide[own].reshape(own_rows * length, spans)) > 0.5
+    first_row = me * own_rows
+    part = first_row // block_rows
+    key_mask = jnp.zeros(key_lane.shape, jnp.float32)
+    for col in range(col_count):
+        mask = crop_ref[slot_at(part, col), pairs:, :]
+        key_mask = key_mask + dot(mask, key_place_ref[col])
+    key_lane[...] = key_mask
+    head_of_lane = lax.broadcasted_iota(jnp.int32, (1, spans), 1) // length
     head_of_row = lax.broadcasted_iota(jnp.int32, (spans, inner), 0) // length
     head_of_channel = lax.broadcasted_iota(jnp.int32, (spans, inner), 1) // head_width
     same_head = (head_of_row == head_of_channel).astype(jnp.float32)
@@ -167,7 +172,8 @@
         scores = lax.dot_general(
             queries[here], tall_keys, (((1,), (1,)), ((), ())), preferred_element_type=jnp.float32
         )
-        scores = jnp.where(allowed[row : row + 1], scores + bias[...], masked_score)
+        allowed = key_lane[pl.ds(first_row - part * block_rows + row, 1), :] > 0.5
+        scores = jnp.where(allowed, scores + bias[...], masked_score)
         top = jnp.zeros_like(scores)
         for head in range(heads):
             here_lanes = head_of_lane == head
@@ -177,8 +183,8 @@
         whole = jnp.zeros_like(scores)
         for head in range(heads):
             here_lanes = head_of_lane == head
-            part = jnp.sum(jnp.where(here_lanes, expo, 0.0), axis=1, keepdims=True)
-            whole = jnp.where(here_lanes, part, whole)
+            amount = jnp.sum(jnp.where(here_lanes, expo, 0.0), axis=1, keepdims=True)
+            whole = jnp.where(here_lanes, amount, whole)
         gathered.append(dot((expo / whole).astype(jnp.bfloat16), tall_values))
     gated = (gating * jnp.concatenate(gathered, axis=0)).astype(jnp.bfloat16)
     residual = residual + dot(gated, attn_outproj_ref[...])
@@ -208,45 +214,50 @@
     block_rows, block_cols, channels = pair_track.shape
     length = block_cols * col_count
     pairs = block_rows * block_cols
+    below = -(-block_rows // 16) * 16
     own_rows = length // devices
-    me = lax.axis_index(crop_axes)
-    in_vmem = pl.BlockSpec(memory_space=pltpu.VMEM)
-    in_smem = pl.BlockSpec(memory_space=pltpu.SMEM)
-    block = pl.pallas_call(
-        pack_kernel,
-        out_shape=jax.ShapeDtypeStruct((pairs + 16, channels), pair_track.dtype),
-        in_specs=[in_vmem, in_vmem],
-        out_specs=in_vmem,
-        name="pack",
-    )(pair_track.reshape(pairs, channels), pair_mask)
+    heads = attn_bias.shape[1]
+    spans = heads * length
+    padded_mask = jnp.pad(pair_mask, ((pairs, below - block_rows), (0, channels - block_cols)))
+    block = jnp.where(
+        lax.broadcasted_iota(jnp.int32, (pairs + below, channels), 0) < pairs,
+        jnp.pad(pair_track.reshape(pairs, channels), ((0, below), (0, 0))),
+        jnp.where(padded_mask > 0, 1, 0).astype(pair_track.dtype),
+    )
     crop = block[None]
-    offsets = [0]
+    slots = [0]
     mask = devices // 2
     while mask:
         turn = mask | 1
         crop = jnp.concatenate(
             [crop, lax.ppermute(crop, crop_axes, [(i, i ^ turn) for i in range(devices)])]
         )
-        offsets = offsets + [offset ^ turn for offset in offsets]
+        slots = slots + [slot ^ turn for slot in slots]
         mask //= 2
-    heads = attn_bias.shape[1]
-    token_col = jnp.broadcast_to(token_mask.astype(jnp.float32)[:, None], (length, lanes))
+    tokens = token_mask.astype(jnp.float32)
+    token_pair = (
+        tokens.reshape(row_count, 1, block_rows, 1) * tokens.reshape(1, col_count, 1, block_cols)
+    ).reshape(devices, block_rows, block_cols)
+    token_pair = jnp.pad(token_pair, ((0, 0), (0, 0), (0, lanes - block_cols)))
+    key_place = (jnp.arange(lanes)[:, None] == jnp.arange(spans)[None, :] % block_cols)[None] & (
+        jnp.arange(col_count)[:, None, None] == (jnp.arange(spans) % length // block_cols)[None, None, :]
+    )
+    key_place = key_place.astype(jnp.bfloat16) * jnp.tile(token_mask, heads).astype(jnp.bfloat16)
     bias_wide = jnp.repeat(attn_bias, length, axis=1)
-    whole = pltpu.VMEM((length, length, channels), jnp.float32)
     flat = pltpu.VMEM((length * length, channels), jnp.float32)
     out = pl.pallas_call(
-        functools.partial(crop_kernel, tuple(offsets), col_count),
+        functools.partial(crop_kernel, tuple(slots), col_count),
         out_shape=jax.ShapeDtypeStruct((own_rows * length, channels), jnp.bfloat16),
-        in_specs=[in_smem, in_smem] + [in_vmem] * 12,
-        out_specs=in_vmem,
-        scratch_shapes=[whole, whole, whole, whole, flat, flat, flat, pltpu.VMEM((length, heads * length), jnp.float32)],
+        in_specs=[pl.BlockSpec(memory_space=pltpu.VMEM)] * 13,
+        out_specs=pl.BlockSpec(memory_space=pltpu.VMEM),
+        scratch_shapes=[flat] * 5
+        + [pltpu.VMEM((length, spans), jnp.float32), pltpu.VMEM((below, spans), jnp.float32)],
         compiler_params=pltpu.CompilerParams(vmem_limit_bytes=48 << 20),
         name="crop",
     )(
-        me.astype(jnp.int32)[None],
-        token_mask,
         crop,
-        token_col,
+        token_pair,
+        key_place,
         mult_gate,
         mult_value,
         mult_outgate,

time: 27.6 us -> 20.8 us (0.75)
  Pallas kernels: 11.6 us -> 5 us
  waiting for transfers between devices: 5.48 us -> 5 us
    pallas_call x2 -> x1, Pallas kernels: 11.6 us -> 5 us  [gathered_crop(): pl.pallas_call(functools.partial(crop_kernel, tuple(slots), col_count), o...]
    unnamed x0 -> x1, other arithmetic: none -> 0.81 us
    concatenate x3, other arithmetic: 0.76 us -> 0.03 us  [gathered_crop(): jnp.concatenate([crop, lax.ppermute(crop, crop_axes, [(i, i ^ turn) for i...]
    ppermute x4, waiting for transfers between devices: 5.48 us -> 5 us  [gathered_crop(): lax.ppermute(crop, crop_axes, [(i, i ^ turn) for i in range(devices)])]
    unnamed x28 -> x25, local copies, waits for them, and re-layouts: 1.41 us -> 1.31 us
  transfers between devices with their start and end apart: 4 -> 4, of which waited for: 4 -> 4; matrix products, arithmetic and copies ran while one was open for 1% -> 2% of each run, Pallas kernels for 0% -> 0%
where the time goes in v2:
time: 20.8 us; the launch traced here: 20.5 us
  starting transfers between devices  7.62 us (37%)
  waiting for transfers between devices  5 us (24%)
  Pallas kernels  5 us (24%)
  local copies, waits for them, and re-layouts  1.64 us (8%)
  other arithmetic  1.01 us (5%)
    ppermute x4, starting transfers between devices, gathered_crop(): lax.ppermute(crop, crop_axes, [(i, i ^ turn) for i in range(devices)])  7.62 us
    ppermute x4, waiting for transfers between devices, gathered_crop(): lax.ppermute(crop, crop_axes, [(i, i ^ turn) for i in range(devices)])  5 us
    pallas_call x1, Pallas kernels, gathered_crop(): pl.pallas_call(functools.partial(crop_kernel, tuple(slots), col_count), o...  5 us
    unnamed x25, local copies, waits for them, and re-layouts  1.31 us
    unnamed x1, other arithmetic  0.81 us
  transfers between devices with their start and end apart: 4, of which 4 were waited for; matrix products, arithmetic and copies ran while one was open for 2% of the time, Pallas kernels for 0%

profile of v2, /device:TPU:0, one launch (start us, length us, event | category | flops | bytes accessed | tf_op | source)
XLA Modules:
  0.0 20.5 jit_solution(3688409914342495840)
XLA Ops:
  0.0 0.8 %constant_dynamic-update-slice_fusion.4 = (bf16[16,80,128]{2,1,0:T(8,128)(2,1)S(1)}, bf16[1,80,128]{2,1,0:T(8,128)(2,1)S(1)}) fusion(s32[8,8]{1,0:T(8,128)} %param.14, bf16[64,128]{1,0:T(8,128)(2,1)} %bitcast.11, pred[80]{0:T(512)(128)(4,1)S(1)} %iota_compare_fusion.2), kind=kLoop, calls=%fused_computation.14 | loop fusion | flops 40959 | bytes 57680
  0.8 3.5 %collective-permute-start = (bf16[1,80,128]{2,1,0:T(8,128)(2,1)S(1)}, bf16[1,80,128]{2,1,0:T(8,128)(2,1)S(1)}, u32[]{:S(2)}, u32[]{:S(2)}) collective-permute-start(bf16[1,80,128]{2,1,0:T(8,128)(2,1)S(1)} %get-tuple-element.6), channel_id=1, source_target_pairs={{0,9},{1,8},{2,11},{3,10},{4,13},{5,12},{6,15},{7,14},{8,1},{9,0},... | collective-permute-start | bytes 61448 | tf_op jit(solution)/shard_map/ppermute | solution.py:233
  4.4 0.0 copy-start.10
  4.4 0.6 %copy-done.10 = s32[32]{0:T(128)S(1)} copy-done((s32[32]{0:T(128)S(1)}, s32[32]{0:T(128)}, u32[]{:S(2)}) %copy-start.10) | copy-done | bytes 152
  5.1 0.1 convert_element_type.25
  5.2 0.1 mul.32
  5.3 0.6 %collective-permute-done = bf16[1,80,128]{2,1,0:T(8,128)(2,1)S(1)} collective-permute-done((bf16[1,80,128]{2,1,0:T(8,128)(2,1)S(1)}, bf16[1,80,128]{2,1,0:T(8,128)(2,1)S(1)}, u32[]{:S(2)}, u32[]{:S(2)}) %collective-permute-start) | collective-permute-done | bytes 20512 | tf_op jit(solution)/shard_map/ppermute | solution.py:233
  5.9 1.9 %collective-permute-start.1 = (bf16[2,80,128]{2,1,0:T(8,128)(2,1)S(1)}, bf16[2,80,128]{2,1,0:T(8,128)(2,1)S(1)}, u32[]{:S(2)}, u32[]{:S(2)}) collective-permute-start(bf16[2,80,128]{2,1,0:T(8,128)(2,1)S(1)} %pad_maximum_fusion.2), channel_id=1, source_target_pairs={{0,5},{1,4},{2,7},{3,6},{4,1},{5,0},{6,3},{7,2},{8,13},{9,12},{10,... | collective-permute-start | bytes 122888 | tf_op jit(solution)/shard_map/ppermute | solution.py:233
  7.8 0.0 copy-start.9
  7.8 0.1 broadcast_multiply_fusion
  7.8 0.6 %copy-done.9 = bf16[128,4]{0,1:T(4,128)(2,1)S(1)} copy-done((bf16[128,4]{0,1:T(4,128)(2,1)S(1)}, bf16[128,4]{0,1:T(4,128)(2,1)}, u32[]{:S(2)}) %copy-start.9) | copy-done | bytes 1048
  8.4 0.1 copy.15.bias_wide_ref
  8.6 0.9 %collective-permute-done.1 = bf16[2,80,128]{2,1,0:T(8,128)(2,1)S(1)} collective-permute-done((bf16[2,80,128]{2,1,0:T(8,128)(2,1)S(1)}, bf16[2,80,128]{2,1,0:T(8,128)(2,1)S(1)}, u32[]{:S(2)}, u32[]{:S(2)}) %collective-permute-start.1) | collective-permute-done | bytes 40992 | tf_op jit(solution)/shard_map/ppermute | solution.py:233
  9.4 1.9 %collective-permute-start.2 = (bf16[4,80,128]{2,1,0:T(8,128)(2,1)S(1)}, bf16[4,80,128]{2,1,0:T(8,128)(2,1)S(1)}, u32[]{:S(2)}, u32[]{:S(2)}) collective-permute-start(bf16[4,80,128]{2,1,0:T(8,128)(2,1)S(1)} %pad_maximum_fusion.1), channel_id=1, source_target_pairs={{0,3},{1,2},{2,1},{3,0},{4,7},{5,6},{6,5},{7,4},{8,11},{9,10},{10,... | collective-permute-start | bytes 245768 | tf_op jit(solution)/shard_map/ppermute | solution.py:233
  11.3 2.5 %collective-permute-done.2 = bf16[4,80,128]{2,1,0:T(8,128)(2,1)S(1)} collective-permute-done((bf16[4,80,128]{2,1,0:T(8,128)(2,1)S(1)}, bf16[4,80,128]{2,1,0:T(8,128)(2,1)S(1)}, u32[]{:S(2)}, u32[]{:S(2)}) %collective-permute-start.2) | collective-permute-done | bytes 81952 | tf_op jit(solution)/shard_map/ppermute | solution.py:233
  13.9 0.0 copy-start.4
  13.9 0.0 copy-start.5
  13.9 0.0 copy-start.7
  13.9 0.0 copy-start.8
  13.9 0.4 %collective-permute-start.3 = (bf16[8,80,128]{2,1,0:T(8,128)(2,1)S(1)}, bf16[8,80,128]{2,1,0:T(8,128)(2,1)S(1)}, u32[]{:S(2)}, u32[]{:S(2)}) collective-permute-start(bf16[8,80,128]{2,1,0:T(8,128)(2,1)S(1)} %pad_maximum_fusion), channel_id=1, source_target_pairs={{0,1},{1,0},{2,3},{3,2},{4,5},{5,4},{6,7},{7,6},{8,9},{9,8},{10,11... | collective-permute-start | bytes 491528 | tf_op jit(solution)/shard_map/ppermute | solution.py:233
  14.2 0.0 copy-start.3
  14.3 0.0 copy-start.2
  14.3 0.0 copy-start
  14.3 0.0 copy-start.1
  14.3 0.0 copy-start.6
  14.3 1.0 %collective-permute-done.3 = bf16[8,80,128]{2,1,0:T(8,128)(2,1)S(1)} collective-permute-done((bf16[8,80,128]{2,1,0:T(8,128)(2,1)S(1)}, bf16[8,80,128]{2,1,0:T(8,128)(2,1)S(1)}, u32[]{:S(2)}, u32[]{:S(2)}) %collective-permute-start.3) | collective-permute-done | bytes 163872 | tf_op jit(solution)/shard_map/ppermute | solution.py:233
  15.4 0.0 copy-done.4
  15.4 0.0 copy-done.5
  15.4 0.0 copy-done.7
  15.4 0.0 copy-done.8
  15.4 0.0 copy-done.3
  15.4 0.0 copy-done.2
  15.4 0.0 copy-done
  15.4 0.0 copy-done.1
  15.5 0.0 copy-done.6
  15.5 5.0 %crop.1 = bf16[64,128]{1,0:T(8,128)(2,1)} custom-call(bf16[16,80,128]{2,1,0:T(8,128)(2,1)S(1)} %constant_dynamic-update-slice_fusion.crop_ref, f32[16,8,128]{2,1,0:T(8,128)S(1)} %pad.14.token_pair_ref, bf16[4,128,128]{2,1,0:T(8,128)(2,1)S(1)} %and_select_fusion.key_place_ref, bf16[128,256]{1,0:T(8,128)(2,1)S(1)} %copy-done.4, ...), custom_call_target="tpu_custom_call" | custom-call | tf_op jit(solution)/shard_map/crop/pallas_call | solution.py:248
  (19 shorter events, 0.2 us)
Async XLA Ops:
  0.8 5.1 %collective-permute-start = (bf16[1,80,128]{2,1,0:T(8,128)(2,1)S(1)}, bf16[1,80,128]{2,1,0:T(8,128)(2,1)S(1)}, u32[]{:S(2)}, u32[]{:S(2)}) collective-permute-start(bf16[1,80,128]{2,1,0:T(8,128)(2,1)S(1)} %get-tuple-element.6), channel_id=1, source_target_pairs={{0,9},{1,8},{2,11},{3,10},{4,13},{5,12},{6,15},{7,14},{8,1},{9,0},... | collective-permute-start | bytes 61448 | tf_op jit(solution)/shard_map/ppermute | solution.py:233
  4.4 0.7 %copy-start.10 = (s32[32]{0:T(128)S(1)}, s32[32]{0:T(128)}, u32[]{:S(2)}) copy-start(s32[32]{0:T(128)} %param.15) | copy-start | bytes 388
  5.9 3.5 %collective-permute-start.1 = (bf16[2,80,128]{2,1,0:T(8,128)(2,1)S(1)}, bf16[2,80,128]{2,1,0:T(8,128)(2,1)S(1)}, u32[]{:S(2)}, u32[]{:S(2)}) collective-permute-start(bf16[2,80,128]{2,1,0:T(8,128)(2,1)S(1)} %pad_maximum_fusion.2), channel_id=1, source_target_pairs={{0,5},{1,4},{2,7},{3,6},{4,1},{5,0},{6,3},{7,2},{8,13},{9,12},{10,... | collective-permute-start | bytes 122888 | tf_op jit(solution)/shard_map/ppermute | solution.py:233
  7.8 0.7 %copy-start.9 = (bf16[128,4]{0,1:T(4,128)(2,1)S(1)}, bf16[128,4]{0,1:T(4,128)(2,1)}, u32[]{:S(2)}) copy-start(bf16[128,4]{0,1:T(4,128)(2,1)} %param.21) | copy-start | bytes 3076
  9.4 4.4 %collective-permute-start.2 = (bf16[4,80,128]{2,1,0:T(8,128)(2,1)S(1)}, bf16[4,80,128]{2,1,0:T(8,128)(2,1)S(1)}, u32[]{:S(2)}, u32[]{:S(2)}) collective-permute-start(bf16[4,80,128]{2,1,0:T(8,128)(2,1)S(1)} %pad_maximum_fusion.1), channel_id=1, source_target_pairs={{0,3},{1,2},{2,1},{3,0},{4,7},{5,6},{6,5},{7,4},{8,11},{9,10},{10,... | collective-permute-start | bytes 245768 | tf_op jit(solution)/shard_map/ppermute | solution.py:233
  13.9 1.5 %copy-start.4 = (bf16[128,256]{1,0:T(8,128)(2,1)S(1)}, bf16[128,256]{1,0:T(8,128)(2,1)}, u32[]{:S(2)}) copy-start(bf16[128,256]{1,0:T(8,128)(2,1)} %mult_gate_ref.1) | copy-start | bytes 196612
  13.9 1.5 %copy-start.5 = (bf16[128,256]{1,0:T(8,128)(2,1)S(1)}, bf16[128,256]{1,0:T(8,128)(2,1)}, u32[]{:S(2)}) copy-start(bf16[128,256]{1,0:T(8,128)(2,1)} %mult_value_ref.1) | copy-start | bytes 196612
  13.9 1.5 %copy-start.7 = (bf16[128,128]{1,0:T(8,128)(2,1)S(1)}, bf16[128,128]{1,0:T(8,128)(2,1)}, u32[]{:S(2)}) copy-start(bf16[128,128]{1,0:T(8,128)(2,1)} %mult_outproj_ref.1) | copy-start | bytes 98308
  13.9 1.5 %copy-start.8 = (bf16[128,128]{1,0:T(8,128)(2,1)S(1)}, bf16[128,128]{1,0:T(8,128)(2,1)}, u32[]{:S(2)}) copy-start(bf16[128,128]{1,0:T(8,128)(2,1)} %attn_outproj_ref.1) | copy-start | bytes 98308
  13.9 1.5 %collective-permute-start.3 = (bf16[8,80,128]{2,1,0:T(8,128)(2,1)S(1)}, bf16[8,80,128]{2,1,0:T(8,128)(2,1)S(1)}, u32[]{:S(2)}, u32[]{:S(2)}) collective-permute-start(bf16[8,80,128]{2,1,0:T(8,128)(2,1)S(1)} %pad_maximum_fusion), channel_id=1, source_target_pairs={{0,1},{1,0},{2,3},{3,2},{4,5},{5,4},{6,7},{7,6},{8,9},{9,8},{10,11... | collective-permute-start | bytes 491528 | tf_op jit(solution)/shard_map/ppermute | solution.py:233
  14.2 1.2 %copy-start.3 = (bf16[512,128]{1,0:T(8,128)(2,1)S(1)}, bf16[512,128]{1,0:T(8,128)(2,1)}, u32[]{:S(2)}) copy-start(bf16[512,128]{1,0:T(8,128)(2,1)} %trans_outproj_ref.1) | copy-start | bytes 393220
  14.3 1.2 %copy-start.2 = (bf16[128,512]{1,0:T(8,128)(2,1)S(1)}, bf16[128,512]{1,0:T(8,128)(2,1)}, u32[]{:S(2)}) copy-start(bf16[128,512]{1,0:T(8,128)(2,1)} %trans_value_ref.1) | copy-start | bytes 393220
  14.3 1.1 %copy-start = (bf16[128,512]{1,0:T(8,128)(2,1)S(1)}, bf16[128,512]{1,0:T(8,128)(2,1)}, u32[]{:S(2)}) copy-start(bf16[128,512]{1,0:T(8,128)(2,1)} %attn_proj_ref.1) | copy-start | bytes 393220
  14.3 1.1 %copy-start.1 = (bf16[128,512]{1,0:T(8,128)(2,1)S(1)}, bf16[128,512]{1,0:T(8,128)(2,1)}, u32[]{:S(2)}) copy-start(bf16[128,512]{1,0:T(8,128)(2,1)} %trans_gate_ref.1) | copy-start | bytes 393220
  14.3 1.1 %copy-start.6 = (bf16[128,128]{1,0:T(8,128)(2,1)S(1)}, bf16[128,128]{1,0:T(8,128)(2,1)}, u32[]{:S(2)}) copy-start(bf16[128,128]{1,0:T(8,128)(2,1)} %mult_outgate_ref.1) | copy-start | bytes 98308

commit v3 on v2

--- a/solution.py
+++ b/solution.py
@@ -42,7 +42,8 @@
 def crop_kernel(
     slots,
     col_count,
-    crop_ref,
+    here_ref,
+    there_ref,
     token_pair_ref,
     key_place_ref,
     mult_gate_ref,
@@ -56,6 +57,7 @@
     trans_value_ref,
     trans_outproj_ref,
     out_ref,
+    crop_ref,
     left,
     right,
     outgate,
@@ -81,7 +83,9 @@
     def slot_at(row, col):
         return slot_index((row * col_count + col) ^ me, devices)
 
-    packed = crop_ref[:, :pairs, :].reshape(whole, channels)
+    crop_ref[: devices // 2] = here_ref[...]
+    crop_ref[devices // 2 :] = there_ref[...]
+    packed = jnp.concatenate([here_ref[:, :pairs, :], there_ref[:, :pairs, :]], axis=0).reshape(whole, channels)
     source = layer_norm(packed.astype(jnp.float32)).astype(jnp.bfloat16)
     diagonal = (
         lax.broadcasted_iota(jnp.int32, (block_cols, lanes), 0)
@@ -89,7 +93,8 @@
     ).astype(jnp.float32)
     masks = []
     for slot, offset in enumerate(slots):
-        mask = crop_ref[slot, pairs:, :].astype(jnp.float32)[:block_rows] * token_pair_ref[me ^ offset]
+        half_ref = (here_ref, there_ref)[slot // (devices // 2)]
+        mask = half_ref[slot % (devices // 2), pairs:, :].astype(jnp.float32)[:block_rows] * token_pair_ref[me ^ offset]
         masks.append((mask[:, None, :] * diagonal[None]).reshape(pairs, lanes))
     mask = dot(jnp.concatenate(masks, axis=0).astype(jnp.bfloat16), jnp.ones((lanes, channels), jnp.bfloat16))
     outgate[...] = sigmoid(dot(source, mult_outgate_ref[...]))
@@ -229,9 +234,11 @@
     mask = devices // 2
     while mask:
         turn = mask | 1
-        crop = jnp.concatenate(
-            [crop, lax.ppermute(crop, crop_axes, [(i, i ^ turn) for i in range(devices)])]
-        )
+        pairing = [(i, i ^ turn) for i in range(devices)]
+        parts = 2 if mask > 1 and crop.shape[0] > 2 else 1
+        arrived = [lax.ppermute(part, crop_axes, pairing) for part in jnp.split(crop, parts)]
+        halves = crop, arrived[0]
+        crop = jnp.concatenate([crop] + arrived)
         slots = slots + [slot ^ turn for slot in slots]
         mask //= 2
     tokens = token_mask.astype(jnp.float32)
@@ -248,14 +255,15 @@
     out = pl.pallas_call(
         functools.partial(crop_kernel, tuple(slots), col_count),
         out_shape=jax.ShapeDtypeStruct((own_rows * length, channels), jnp.bfloat16),
-        in_specs=[pl.BlockSpec(memory_space=pltpu.VMEM)] * 13,
+        in_specs=[pl.BlockSpec(memory_space=pltpu.VMEM)] * 14,
         out_specs=pl.BlockSpec(memory_space=pltpu.VMEM),
-        scratch_shapes=[flat] * 5
+        scratch_shapes=[pltpu.VMEM((devices,) + halves[0].shape[1:], halves[0].dtype)]
+        + [flat] * 5
         + [pltpu.VMEM((length, spans), jnp.float32), pltpu.VMEM((below, spans), jnp.float32)],
         compiler_params=pltpu.CompilerParams(vmem_limit_bytes=48 << 20),
         name="crop",
     )(
-        crop,
+        *halves,
         token_pair,
         key_place,
         mult_gate,

time: 20.8 us -> 20.2 us (0.971)
  waiting for transfers between devices: 5 us -> 3.15 us
  starting transfers between devices: 7.62 us -> 8.98 us
    ppermute x4 -> x5, waiting for transfers between devices: 5 us -> 3.15 us  [gathered_crop(): lax.ppermute(part, crop_axes, pairing)]
    ppermute x4 -> x5, starting transfers between devices: 7.62 us -> 8.98 us  [gathered_crop(): lax.ppermute(part, crop_axes, pairing)]
  transfers between devices with their start and end apart: 4 -> 5, of which waited for: 4 -> 4; matrix products, arithmetic and copies ran while one was open for 2% -> 2% of each run, Pallas kernels for 0% -> 0%
where the time goes in v3:
time: 20.2 us; the launch traced here: 19.9 us
  starting transfers between devices  8.98 us (44%)
  Pallas kernels  5.01 us (25%)
  waiting for transfers between devices  3.15 us (16%)
  local copies, waits for them, and re-layouts  1.62 us (8%)
  other arithmetic  0.98 us (5%)
    ppermute x5, starting transfers between devices, gathered_crop(): lax.ppermute(part, crop_axes, pairing)  8.98 us
    pallas_call x1, Pallas kernels, gathered_crop(): pl.pallas_call(functools.partial(crop_kernel, tuple(slots), col_count), o...  5.01 us
    ppermute x5, waiting for transfers between devices, gathered_crop(): lax.ppermute(part, crop_axes, pairing)  3.15 us
    unnamed x25, local copies, waits for them, and re-layouts  1.31 us
    unnamed x1, other arithmetic  0.81 us
  transfers between devices with their start and end apart: 5, of which 4 were waited for; matrix products, arithmetic and copies ran while one was open for 2% of the time, Pallas kernels for 0%

profile of v3, /device:TPU:0, one launch (start us, length us, event | category | flops | bytes accessed | tf_op | source)
XLA Modules:
  0.0 19.9 jit_solution(5943121763444448509)
XLA Ops:
  0.0 0.8 %constant_dynamic-update-slice_fusion.4 = (bf16[8,80,128]{2,1,0:T(8,128)(2,1)S(1)}, bf16[1,80,128]{2,1,0:T(8,128)(2,1)S(1)}) fusion(s32[8,8]{1,0:T(8,128)} %param.14, bf16[64,128]{1,0:T(8,128)(2,1)} %bitcast.11, pred[80]{0:T(512)(128)(4,1)S(1)} %iota_compare_fusion.2), kind=kLoop, calls=%fused_computation.12 | loop fusion | flops 40959 | bytes 57680
  0.8 3.5 %collective-permute-start = (bf16[1,80,128]{2,1,0:T(8,128)(2,1)S(1)}, bf16[1,80,128]{2,1,0:T(8,128)(2,1)S(1)}, u32[]{:S(2)}, u32[]{:S(2)}) collective-permute-start(bf16[1,80,128]{2,1,0:T(8,128)(2,1)S(1)} %get-tuple-element.6), channel_id=1, source_target_pairs={{0,9},{1,8},{2,11},{3,10},{4,13},{5,12},{6,15},{7,14},{8,1},{9,0},... | collective-permute-start | bytes 61448 | tf_op jit(solution)/shard_map/ppermute | solution.py:239
  4.4 0.0 copy-start.10
  4.4 0.6 %copy-done.10 = s32[32]{0:T(128)S(1)} copy-done((s32[32]{0:T(128)S(1)}, s32[32]{0:T(128)}, u32[]{:S(2)}) %copy-start.10) | copy-done | bytes 152
  5.0 0.1 mul.32
  5.2 0.0 copy-start.8
  5.2 0.1 broadcast_multiply_fusion
  5.3 0.0 copy-start.9
  5.3 0.1 convert_element_type.25
  5.4 0.6 %copy-done.9 = bf16[128,4]{0,1:T(4,128)(2,1)S(1)} copy-done((bf16[128,4]{0,1:T(4,128)(2,1)S(1)}, bf16[128,4]{0,1:T(4,128)(2,1)}, u32[]{:S(2)}) %copy-start.9) | copy-done | bytes 1048
  6.0 0.0 copy-start.7
  6.0 0.0 copy-start.5
  6.0 0.1 copy.15.bias_wide_ref
  6.1 0.0 copy-start.3
  6.1 0.0 collective-permute-done
  6.1 0.0 copy-start.4
  6.2 1.9 %collective-permute-start.1 = (bf16[2,80,128]{2,1,0:T(8,128)(2,1)S(1)}, bf16[2,80,128]{2,1,0:T(8,128)(2,1)S(1)}, u32[]{:S(2)}, u32[]{:S(2)}) collective-permute-start(bf16[2,80,128]{2,1,0:T(8,128)(2,1)S(1)} %pad_maximum_fusion), channel_id=1, source_target_pairs={{0,5},{1,4},{2,7},{3,6},{4,1},{5,0},{6,3},{7,2},{8,13},{9,12},{10,... | collective-permute-start | bytes 122888 | tf_op jit(solution)/shard_map/ppermute | solution.py:239
  8.1 1.2 %collective-permute-start.2 = (bf16[2,80,128]{2,1,0:T(8,128)(2,1)S(1)}, bf16[2,80,128]{2,1,0:T(8,128)(2,1)S(1)}, u32[]{:S(2)}, u32[]{:S(2)}) collective-permute-start(bf16[2,80,128]{2,1,0:T(8,128)(2,1)S(1)} %pad_maximum_fusion), channel_id=1, source_target_pairs={{0,3},{1,2},{2,1},{3,0},{4,7},{5,6},{6,5},{7,4},{8,11},{9,10},{10,... | collective-permute-start | bytes 122888 | tf_op jit(solution)/shard_map/ppermute | solution.py:239
  9.3 0.0 copy-start.6
  9.3 0.4 %collective-permute-done.1 = bf16[2,80,128]{2,1,0:T(8,128)(2,1)S(1)} collective-permute-done((bf16[2,80,128]{2,1,0:T(8,128)(2,1)S(1)}, bf16[2,80,128]{2,1,0:T(8,128)(2,1)S(1)}, u32[]{:S(2)}, u32[]{:S(2)}) %collective-permute-start.1) | collective-permute-done | bytes 40992 | tf_op jit(solution)/shard_map/ppermute | solution.py:239
  9.8 1.7 %collective-permute-start.3 = (bf16[2,80,128]{2,1,0:T(8,128)(2,1)S(1)}, bf16[2,80,128]{2,1,0:T(8,128)(2,1)S(1)}, u32[]{:S(2)}, u32[]{:S(2)}) collective-permute-start(bf16[2,80,128]{2,1,0:T(8,128)(2,1)S(1)} %collective-permute-done.1), channel_id=1, source_target_pairs={{0,3},{1,2},{2,1},{3,0},{4,7},{5,6},{6,5},{7,4},{8,11},{9,10},{10,... | collective-permute-start | bytes 122888 | tf_op jit(solution)/shard_map/ppermute | solution.py:239
  11.4 0.0 copy-start.2
  11.4 0.2 collective-permute-done.2
  11.6 0.0 copy-start.1
  11.6 0.0 copy-start
  11.7 1.6 %collective-permute-done.3 = bf16[2,80,128]{2,1,0:T(8,128)(2,1)S(1)} collective-permute-done((bf16[2,80,128]{2,1,0:T(8,128)(2,1)S(1)}, bf16[2,80,128]{2,1,0:T(8,128)(2,1)S(1)}, u32[]{:S(2)}, u32[]{:S(2)}) %collective-permute-start.3) | collective-permute-done | bytes 40992 | tf_op jit(solution)/shard_map/ppermute | solution.py:239
  13.2 0.6 %collective-permute-start.4 = (bf16[8,80,128]{2,1,0:T(8,128)(2,1)S(1)}, bf16[8,80,128]{2,1,0:T(8,128)(2,1)S(1)}, u32[]{:S(2)}, u32[]{:S(2)}) collective-permute-start(bf16[8,80,128]{2,1,0:T(8,128)(2,1)S(1)} %constant_dynamic-update-slice_fusion.here_ref), channel_id=1, source_target_pairs={{0,1},{1,0},{2,3},{3,2},{4,5},{5,4},{6,7},{7,6},{8,9},{9,8},{10,11... | collective-permute-start | bytes 491528 | tf_op jit(solution)/shard_map/ppermute | solution.py:239
  13.9 1.0 %collective-permute-done.4.there_ref = bf16[8,80,128]{2,1,0:T(8,128)(2,1)S(1)} collective-permute-done((bf16[8,80,128]{2,1,0:T(8,128)(2,1)S(1)}, bf16[8,80,128]{2,1,0:T(8,128)(2,1)S(1)}, u32[]{:S(2)}, u32[]{:S(2)}) %collective-permute-start.4) | collective-permute-done | bytes 163872 | tf_op jit(solution)/shard_map/ppermute | solution.py:239
  14.9 0.0 copy-done.8
  14.9 0.0 copy-done.7
  14.9 0.0 copy-done.5
  14.9 0.0 copy-done.3
  14.9 0.0 copy-done.4
  14.9 0.0 copy-done.6
  14.9 0.0 copy-done.2
  14.9 0.0 copy-done.1
  14.9 0.0 copy-done
  14.9 5.0 %crop.1 = bf16[64,128]{1,0:T(8,128)(2,1)} custom-call(bf16[8,80,128]{2,1,0:T(8,128)(2,1)S(1)} %constant_dynamic-update-slice_fusion.here_ref, bf16[8,80,128]{2,1,0:T(8,128)(2,1)S(1)} %collective-permute-done.4.there_ref, f32[16,8,128]{2,1,0:T(8,128)S(1)} %pad.14.token_pair_ref, bf16[4,128,128]{2,1,0:T(8,128)(2,1)S(1)} %and_select_fusion.key_place_ref, ...), custom_call_target="tpu_custom_call" | custom-call | tf_op jit(solution)/shard_map/crop/pallas_call | solution.py:255
  (17 shorter events, 0.2 us)
Async XLA Ops:
  0.8 5.3 %collective-permute-start = (bf16[1,80,128]{2,1,0:T(8,128)(2,1)S(1)}, bf16[1,80,128]{2,1,0:T(8,128)(2,1)S(1)}, u32[]{:S(2)}, u32[]{:S(2)}) collective-permute-start(bf16[1,80,128]{2,1,0:T(8,128)(2,1)S(1)} %get-tuple-element.6), channel_id=1, source_target_pairs={{0,9},{1,8},{2,11},{3,10},{4,13},{5,12},{6,15},{7,14},{8,1},{9,0},... | collective-permute-start | bytes 61448 | tf_op jit(solution)/shard_map/ppermute | solution.py:239
  4.4 0.7 %copy-start.10 = (s32[32]{0:T(128)S(1)}, s32[32]{0:T(128)}, u32[]{:S(2)}) copy-start(s32[32]{0:T(128)} %param.15) | copy-start | bytes 388
  5.2 9.7 %copy-start.8 = (bf16[128,128]{1,0:T(8,128)(2,1)S(1)}, bf16[128,128]{1,0:T(8,128)(2,1)}, u32[]{:S(2)}) copy-start(bf16[128,128]{1,0:T(8,128)(2,1)} %attn_outproj_ref.1) | copy-start | bytes 98308
  5.3 0.7 %copy-start.9 = (bf16[128,4]{0,1:T(4,128)(2,1)S(1)}, bf16[128,4]{0,1:T(4,128)(2,1)}, u32[]{:S(2)}) copy-start(bf16[128,4]{0,1:T(4,128)(2,1)} %param.21) | copy-start | bytes 3076
  6.0 8.9 %copy-start.7 = (bf16[128,128]{1,0:T(8,128)(2,1)S(1)}, bf16[128,128]{1,0:T(8,128)(2,1)}, u32[]{:S(2)}) copy-start(bf16[128,128]{1,0:T(8,128)(2,1)} %mult_outproj_ref.1) | copy-start | bytes 98308
  6.0 8.9 %copy-start.5 = (bf16[128,256]{1,0:T(8,128)(2,1)S(1)}, bf16[128,256]{1,0:T(8,128)(2,1)}, u32[]{:S(2)}) copy-start(bf16[128,256]{1,0:T(8,128)(2,1)} %mult_value_ref.1) | copy-start | bytes 196612
  6.1 8.8 %copy-start.3 = (bf16[512,128]{1,0:T(8,128)(2,1)S(1)}, bf16[512,128]{1,0:T(8,128)(2,1)}, u32[]{:S(2)}) copy-start(bf16[512,128]{1,0:T(8,128)(2,1)} %trans_outproj_ref.1) | copy-start | bytes 393220
  6.1 8.7 %copy-start.4 = (bf16[128,256]{1,0:T(8,128)(2,1)S(1)}, bf16[128,256]{1,0:T(8,128)(2,1)}, u32[]{:S(2)}) copy-start(bf16[128,256]{1,0:T(8,128)(2,1)} %mult_gate_ref.1) | copy-start | bytes 196612
  6.2 3.6 %collective-permute-start.1 = (bf16[2,80,128]{2,1,0:T(8,128)(2,1)S(1)}, bf16[2,80,128]{2,1,0:T(8,128)(2,1)S(1)}, u32[]{:S(2)}, u32[]{:S(2)}) collective-permute-start(bf16[2,80,128]{2,1,0:T(8,128)(2,1)S(1)} %pad_maximum_fusion), channel_id=1, source_target_pairs={{0,5},{1,4},{2,7},{3,6},{4,1},{5,0},{6,3},{7,2},{8,13},{9,12},{10,... | collective-permute-start | bytes 122888 | tf_op jit(solution)/shard_map/ppermute | solution.py:239
  8.1 3.5 %collective-permute-start.2 = (bf16[2,80,128]{2,1,0:T(8,128)(2,1)S(1)}, bf16[2,80,128]{2,1,0:T(8,128)(2,1)S(1)}, u32[]{:S(2)}, u32[]{:S(2)}) collective-permute-start(bf16[2,80,128]{2,1,0:T(8,128)(2,1)S(1)} %pad_maximum_fusion), channel_id=1, source_target_pairs={{0,3},{1,2},{2,1},{3,0},{4,7},{5,6},{6,5},{7,4},{8,11},{9,10},{10,... | collective-permute-start | bytes 122888 | tf_op jit(solution)/shard_map/ppermute | solution.py:239
  9.3 5.6 %copy-start.6 = (bf16[128,128]{1,0:T(8,128)(2,1)S(1)}, bf16[128,128]{1,0:T(8,128)(2,1)}, u32[]{:S(2)}) copy-start(bf16[128,128]{1,0:T(8,128)(2,1)} %mult_outgate_ref.1) | copy-start | bytes 98308
  9.8 3.4 %collective-permute-start.3 = (bf16[2,80,128]{2,1,0:T(8,128)(2,1)S(1)}, bf16[2,80,128]{2,1,0:T(8,128)(2,1)S(1)}, u32[]{:S(2)}, u32[]{:S(2)}) collective-permute-start(bf16[2,80,128]{2,1,0:T(8,128)(2,1)S(1)} %collective-permute-done.1), channel_id=1, source_target_pairs={{0,3},{1,2},{2,1},{3,0},{4,7},{5,6},{6,5},{7,4},{8,11},{9,10},{10,... | collective-permute-start | bytes 122888 | tf_op jit(solution)/shard_map/ppermute | solution.py:239
  11.4 3.5 %copy-start.2 = (bf16[128,512]{1,0:T(8,128)(2,1)S(1)}, bf16[128,512]{1,0:T(8,128)(2,1)}, u32[]{:S(2)}) copy-start(bf16[128,512]{1,0:T(8,128)(2,1)} %trans_value_ref.1) | copy-start | bytes 393220
  11.6 3.3 %copy-start.1 = (bf16[128,512]{1,0:T(8,128)(2,1)S(1)}, bf16[128,512]{1,0:T(8,128)(2,1)}, u32[]{:S(2)}) copy-start(bf16[128,512]{1,0:T(8,128)(2,1)} %trans_gate_ref.1) | copy-start | bytes 393220
  11.6 3.3 %copy-start = (bf16[128,512]{1,0:T(8,128)(2,1)S(1)}, bf16[128,512]{1,0:T(8,128)(2,1)}, u32[]{:S(2)}) copy-start(bf16[128,512]{1,0:T(8,128)(2,1)} %attn_proj_ref.1) | copy-start | bytes 393220
  13.2 1.6 %collective-permute-start.4 = (bf16[8,80,128]{2,1,0:T(8,128)(2,1)S(1)}, bf16[8,80,128]{2,1,0:T(8,128)(2,1)S(1)}, u32[]{:S(2)}, u32[]{:S(2)}) collective-permute-start(bf16[8,80,128]{2,1,0:T(8,128)(2,1)S(1)} %constant_dynamic-update-slice_fusion.here_ref), channel_id=1, source_target_pairs={{0,1},{1,0},{2,3},{3,2},{4,5},{5,4},{6,7},{7,6},{8,9},{9,8},{10,11... | collective-permute-start | bytes 491528 | tf_op jit(solution)/shard_map/ppermute | solution.py:239

commit v4 on v3

--- a/solution.py
+++ b/solution.py
@@ -19,7 +19,7 @@
 
 
 def sigmoid(values):
-    return 1.0 / (1.0 + jnp.exp(-values))
+    return 0.5 * jnp.tanh(0.5 * values) + 0.5
 
 
 def layer_norm(values):
@@ -51,7 +51,7 @@
     mult_outgate_ref,
     mult_outproj_ref,
     attn_proj_ref,
-    bias_wide_ref,
+    attn_bias_ref,
     attn_outproj_ref,
     trans_gate_ref,
     trans_value_ref,
@@ -62,15 +62,15 @@
     right,
     outgate,
     product,
-    after,
     bias,
     key_lane,
+    bias_wide_ref,
 ):
-    channels = after.shape[1]
+    channels = outgate.shape[1]
     hidden = mult_outproj_ref.shape[0]
     inner = attn_outproj_ref.shape[0]
     length, spans = bias.shape
-    heads = spans // length
+    heads = attn_bias_ref.shape[0]
     head_width = inner // heads
     own_rows = out_ref.shape[0] // length
     devices = len(slots)
@@ -91,6 +91,16 @@
         lax.broadcasted_iota(jnp.int32, (block_cols, lanes), 0)
         == lax.broadcasted_iota(jnp.int32, (block_cols, lanes), 1)
     ).astype(jnp.float32)
+    head_lanes = (
+        lax.broadcasted_iota(jnp.int32, (heads, spans), 0)
+        == lax.broadcasted_iota(jnp.int32, (heads, spans), 1) // length
+    ).astype(jnp.float32)
+    bias_wide_ref[...] = lax.dot_general(
+        attn_bias_ref[...].astype(jnp.float32),
+        head_lanes,
+        (((0,), (0,)), ((), ())),
+        preferred_element_type=jnp.float32,
+    ).astype(jnp.bfloat16)
     masks = []
     for slot, offset in enumerate(slots):
         half_ref = (here_ref, there_ref)[slot // (devices // 2)]
@@ -108,11 +118,10 @@
 
     starts = [[slot_at(row, col) * pairs for col in range(col_count)] for row in range(row_count)]
 
-    @pl.loop(0, row_count)
-    def _(part):
+    for part in range(row_count):
         total = [jnp.zeros((length, hidden), jnp.float32) for _ in range(block_rows)]
         for col in range(col_count):
-            start = slot_at(part, col) * pairs
+            start = starts[part][col]
             for k in range(block_cols):
                 column = jnp.concatenate(
                     [
@@ -137,38 +146,56 @@
             axis=0,
         ).reshape(whole, channels)
 
-    crossed = product[...].astype(jnp.bfloat16).astype(jnp.float32)
-    mixed = layer_norm(crossed).astype(jnp.bfloat16)
-    gate = absolute(lambda row, col: outgate[pl.ds(pl.multiple_of(starts[row][col], pairs), pairs), :])
-    track = absolute(lambda row, col: crop_ref[slot_at(row, col), :pairs, :].astype(jnp.float32))
-    summed = track + gate * dot(mixed, mult_outproj_ref[...])
-    after[...] = summed
-    again = layer_norm(summed)
-    product[...] = again
-    key_of_lane = lax.broadcasted_iota(jnp.int32, (length, spans), 1) % length
-    on_key = (lax.broadcasted_iota(jnp.int32, (length, spans), 0) == key_of_lane).astype(jnp.float32)
-    wide = dot(again.astype(jnp.bfloat16), bias_wide_ref[...]).astype(jnp.bfloat16).astype(jnp.float32)
-    bias[...] = jnp.sum(wide.reshape(length, length, spans) * on_key[None], axis=1)
-
-    own = pl.ds(pl.multiple_of(me * own_rows * length, own_rows * length), own_rows * length)
-    residual = after[own, :]
-    source = product[own, :].astype(jnp.bfloat16)
+    def grown(rows, track, gate):
+        mixed = layer_norm(rows.astype(jnp.bfloat16).astype(jnp.float32)).astype(jnp.bfloat16)
+        rows = track + gate * dot(mixed, mult_outproj_ref[...])
+        return rows, layer_norm(rows).astype(jnp.bfloat16)
+
+    first_row = me * own_rows
+    part = first_row // block_rows
+    first_own = first_row - part * block_rows
+    own_pairs = own_rows * block_cols
+    inside = pl.ds(pl.multiple_of(first_own * block_cols, own_pairs), own_pairs)
+    own_slots = [slot_at(part, col) for col in range(col_count)]
+
+    def own_block(values):
+        values = [value.reshape(own_rows, block_cols, channels) for value in values]
+        return jnp.concatenate(values, axis=1).reshape(own_rows * length, channels)
+
+    residual, source = grown(
+        product[pl.ds(pl.multiple_of(me * own_rows * length, own_rows * length), own_rows * length), :],
+        own_block([crop_ref[slot, inside, :].astype(jnp.float32) for slot in own_slots]),
+        own_block(
+            [
+                outgate[pl.ds(pl.multiple_of(slot * pairs + first_own * block_cols, own_pairs), own_pairs), :]
+                for slot in own_slots
+            ]
+        ),
+    )
     projected = dot(source, attn_proj_ref[...])
     queries = (projected[:, :inner] * head_width ** (-0.5)).astype(jnp.bfloat16)
     keys = projected[:, inner : 2 * inner]
     values = projected[:, 2 * inner : 3 * inner]
     gating = sigmoid(projected[:, 3 * inner :])
-    first_row = me * own_rows
-    part = first_row // block_rows
     key_mask = jnp.zeros(key_lane.shape, jnp.float32)
     for col in range(col_count):
-        mask = crop_ref[slot_at(part, col), pairs:, :]
+        mask = crop_ref[own_slots[col], pairs:, :]
         key_mask = key_mask + dot(mask, key_place_ref[col])
     key_lane[...] = key_mask
     head_of_lane = lax.broadcasted_iota(jnp.int32, (1, spans), 1) // length
     head_of_row = lax.broadcasted_iota(jnp.int32, (spans, inner), 0) // length
     head_of_channel = lax.broadcasted_iota(jnp.int32, (spans, inner), 1) // head_width
     same_head = (head_of_row == head_of_channel).astype(jnp.float32)
+    _, again = grown(
+        product[...],
+        absolute(lambda row, col: crop_ref[slot_at(row, col), :pairs, :].astype(jnp.float32)),
+        absolute(lambda row, col: outgate[pl.ds(pl.multiple_of(starts[row][col], pairs), pairs), :]),
+    )
+    key_of_lane = lax.broadcasted_iota(jnp.int32, (length, spans), 1) % length
+    on_key = (lax.broadcasted_iota(jnp.int32, (length, spans), 0) == key_of_lane).astype(jnp.float32)
+    wide = dot(again, bias_wide_ref[...]).astype(jnp.bfloat16).astype(jnp.float32)
+    bias[...] = jnp.sum(wide.reshape(length, length, spans) * on_key[None], axis=1)
+
     gathered = []
     for row in range(own_rows):
         here = slice(row * length, (row + 1) * length)
@@ -177,7 +204,7 @@
         scores = lax.dot_general(
             queries[here], tall_keys, (((1,), (1,)), ((), ())), preferred_element_type=jnp.float32
         )
-        allowed = key_lane[pl.ds(first_row - part * block_rows + row, 1), :] > 0.5
+        allowed = key_lane[pl.ds(first_own + row, 1), :] > 0.5
         scores = jnp.where(allowed, scores + bias[...], masked_score)
         top = jnp.zeros_like(scores)
         for head in range(heads):
@@ -250,16 +277,17 @@
         jnp.arange(col_count)[:, None, None] == (jnp.arange(spans) % length // block_cols)[None, None, :]
     )
     key_place = key_place.astype(jnp.bfloat16) * jnp.tile(token_mask, heads).astype(jnp.bfloat16)
-    bias_wide = jnp.repeat(attn_bias, length, axis=1)
     flat = pltpu.VMEM((length * length, channels), jnp.float32)
+    tall = pltpu.VMEM((length * length + pairs, channels), jnp.float32)
     out = pl.pallas_call(
         functools.partial(crop_kernel, tuple(slots), col_count),
         out_shape=jax.ShapeDtypeStruct((own_rows * length, channels), jnp.bfloat16),
         in_specs=[pl.BlockSpec(memory_space=pltpu.VMEM)] * 14,
         out_specs=pl.BlockSpec(memory_space=pltpu.VMEM),
         scratch_shapes=[pltpu.VMEM((devices,) + halves[0].shape[1:], halves[0].dtype)]
-        + [flat] * 5
-        + [pltpu.VMEM((length, spans), jnp.float32), pltpu.VMEM((below, spans), jnp.float32)],
+        + [flat, tall, flat, flat]
+        + [pltpu.VMEM((length, spans), jnp.float32), pltpu.VMEM((below, spans), jnp.float32)]
+        + [pltpu.VMEM((channels, spans), jnp.bfloat16)],
         compiler_params=pltpu.CompilerParams(vmem_limit_bytes=48 << 20),
         name="crop",
     )(
@@ -271,7 +299,7 @@
         mult_outgate,
         mult_outproj,
         attn_proj,
-        bias_wide,
+        attn_bias.T,
         attn_outproj,
         trans_gate,
         trans_value,
@@ -393,7 +421,8 @@
     heads = others[7].shape[1]
     length = pair_track.shape[1] * lax.axis_size("col")
     fits = pairs * pair_track.shape[2] * 4 <= crop_bytes_max
-    if fits and heads * length == lanes and pair_track.shape[2] == lanes and devices & (devices - 1) == 0:
+    tiled = length // devices * pair_track.shape[1] % 16 == 0
+    if fits and tiled and heads * length == lanes and pair_track.shape[2] == lanes and devices & (devices - 1) == 0:
         return gathered_crop(pair_track, *others)
     return split_crop(pair_track, *others)
 

time: 20.2 us -> 19.8 us (0.980)
  local copies, waits for them, and re-layouts: 1.62 us -> 0.92 us
  starting transfers between devices: 8.98 us -> 9.3 us
    unnamed x25, local copies, waits for them, and re-layouts: 1.31 us -> 0.73 us
    ppermute x5, starting transfers between devices: 8.98 us -> 9.3 us  [gathered_crop(): lax.ppermute(part, crop_axes, pairing)]
where the time goes in v4:
time: 19.8 us; the launch traced here: 19.6 us
  starting transfers between devices  9.3 us (47%)
  Pallas kernels  4.95 us (25%)
  waiting for transfers between devices  3.23 us (16%)
  other arithmetic  0.98 us (5%)
  local copies, waits for them, and re-layouts  0.92 us (5%)
    ppermute x5, starting transfers between devices, gathered_crop(): lax.ppermute(part, crop_axes, pairing)  9.3 us
    pallas_call x1, Pallas kernels, gathered_crop(): pl.pallas_call(functools.partial(crop_kernel, tuple(slots), col_count), o...  4.95 us
    ppermute x5, waiting for transfers between devices, gathered_crop(): lax.ppermute(part, crop_axes, pairing)  3.23 us
    unnamed x1, other arithmetic  0.81 us
    unnamed x25, local copies, waits for them, and re-layouts  0.73 us
  transfers between devices with their start and end apart: 5, of which 4 were waited for; matrix products, arithmetic and copies ran while one was open for 2% of the time, Pallas kernels for 0%

profile of v4, /device:TPU:0, one launch (start us, length us, event | category | flops | bytes accessed | tf_op | source)
XLA Modules:
  0.0 19.6 jit_solution(12344077384593346974)
XLA Ops:
  0.0 0.8 %constant_dynamic-update-slice_fusion.4 = (bf16[8,80,128]{2,1,0:T(8,128)(2,1)S(1)}, bf16[1,80,128]{2,1,0:T(8,128)(2,1)S(1)}) fusion(s32[8,8]{1,0:T(8,128)} %param.14, bf16[64,128]{1,0:T(8,128)(2,1)} %bitcast.11, pred[80]{0:T(512)(128)(4,1)S(1)} %iota_compare_fusion.2), kind=kLoop, calls=%fused_computation.12 | loop fusion | flops 40959 | bytes 57680
  0.8 3.5 %collective-permute-start = (bf16[1,80,128]{2,1,0:T(8,128)(2,1)S(1)}, bf16[1,80,128]{2,1,0:T(8,128)(2,1)S(1)}, u32[]{:S(2)}, u32[]{:S(2)}) collective-permute-start(bf16[1,80,128]{2,1,0:T(8,128)(2,1)S(1)} %get-tuple-element.6), channel_id=1, source_target_pairs={{0,9},{1,8},{2,11},{3,10},{4,13},{5,12},{6,15},{7,14},{8,1},{9,0},... | collective-permute-start | bytes 61448 | tf_op jit(solution)/shard_map/ppermute | solution.py:266
  4.4 0.0 copy-start.10
  4.4 0.6 %copy-done.10 = s32[32]{0:T(128)S(1)} copy-done((s32[32]{0:T(128)S(1)}, s32[32]{0:T(128)}, u32[]{:S(2)}) %copy-start.10) | copy-done | bytes 152
  5.0 0.1 mul.32
  5.1 0.0 copy-start.9
  5.2 0.0 copy-start.8
  5.2 0.0 copy-start.5
  5.2 0.0 copy-start.7
  5.2 0.1 broadcast_multiply_fusion
  5.3 0.1 convert_element_type.25
  5.4 0.0 copy-start.3
  5.4 0.5 %collective-permute-done = bf16[1,80,128]{2,1,0:T(8,128)(2,1)S(1)} collective-permute-done((bf16[1,80,128]{2,1,0:T(8,128)(2,1)S(1)}, bf16[1,80,128]{2,1,0:T(8,128)(2,1)S(1)}, u32[]{:S(2)}, u32[]{:S(2)}) %collective-permute-start) | collective-permute-done | bytes 20512 | tf_op jit(solution)/shard_map/ppermute | solution.py:266
  5.9 0.0 copy-start.4
  5.9 1.9 %collective-permute-start.1 = (bf16[2,80,128]{2,1,0:T(8,128)(2,1)S(1)}, bf16[2,80,128]{2,1,0:T(8,128)(2,1)S(1)}, u32[]{:S(2)}, u32[]{:S(2)}) collective-permute-start(bf16[2,80,128]{2,1,0:T(8,128)(2,1)S(1)} %pad_maximum_fusion), channel_id=1, source_target_pairs={{0,5},{1,4},{2,7},{3,6},{4,1},{5,0},{6,3},{7,2},{8,13},{9,12},{10,... | collective-permute-start | bytes 122888 | tf_op jit(solution)/shard_map/ppermute | solution.py:266
  7.8 1.5 %collective-permute-start.2 = (bf16[2,80,128]{2,1,0:T(8,128)(2,1)S(1)}, bf16[2,80,128]{2,1,0:T(8,128)(2,1)S(1)}, u32[]{:S(2)}, u32[]{:S(2)}) collective-permute-start(bf16[2,80,128]{2,1,0:T(8,128)(2,1)S(1)} %pad_maximum_fusion), channel_id=1, source_target_pairs={{0,3},{1,2},{2,1},{3,0},{4,7},{5,6},{6,5},{7,4},{8,11},{9,10},{10,... | collective-permute-start | bytes 122888 | tf_op jit(solution)/shard_map/ppermute | solution.py:266
  9.3 0.0 copy-start.6
  9.4 0.2 collective-permute-done.1
  9.5 1.8 %collective-permute-start.3 = (bf16[2,80,128]{2,1,0:T(8,128)(2,1)S(1)}, bf16[2,80,128]{2,1,0:T(8,128)(2,1)S(1)}, u32[]{:S(2)}, u32[]{:S(2)}) collective-permute-start(bf16[2,80,128]{2,1,0:T(8,128)(2,1)S(1)} %collective-permute-done.1), channel_id=1, source_target_pairs={{0,3},{1,2},{2,1},{3,0},{4,7},{5,6},{6,5},{7,4},{8,11},{9,10},{10,... | collective-permute-start | bytes 122888 | tf_op jit(solution)/shard_map/ppermute | solution.py:266
  11.3 0.0 copy-start.2
  11.3 0.0 collective-permute-done.2
  11.3 0.0 copy-start.1
  11.4 0.0 copy-start
  11.4 1.6 %collective-permute-done.3 = bf16[2,80,128]{2,1,0:T(8,128)(2,1)S(1)} collective-permute-done((bf16[2,80,128]{2,1,0:T(8,128)(2,1)S(1)}, bf16[2,80,128]{2,1,0:T(8,128)(2,1)S(1)}, u32[]{:S(2)}, u32[]{:S(2)}) %collective-permute-start.3) | collective-permute-done | bytes 40992 | tf_op jit(solution)/shard_map/ppermute | solution.py:266
  13.0 0.5 %collective-permute-start.4 = (bf16[8,80,128]{2,1,0:T(8,128)(2,1)S(1)}, bf16[8,80,128]{2,1,0:T(8,128)(2,1)S(1)}, u32[]{:S(2)}, u32[]{:S(2)}) collective-permute-start(bf16[8,80,128]{2,1,0:T(8,128)(2,1)S(1)} %constant_dynamic-update-slice_fusion.here_ref), channel_id=1, source_target_pairs={{0,1},{1,0},{2,3},{3,2},{4,5},{5,4},{6,7},{7,6},{8,9},{9,8},{10,11... | collective-permute-start | bytes 491528 | tf_op jit(solution)/shard_map/ppermute | solution.py:266
  13.6 1.0 %collective-permute-done.4.there_ref = bf16[8,80,128]{2,1,0:T(8,128)(2,1)S(1)} collective-permute-done((bf16[8,80,128]{2,1,0:T(8,128)(2,1)S(1)}, bf16[8,80,128]{2,1,0:T(8,128)(2,1)S(1)}, u32[]{:S(2)}, u32[]{:S(2)}) %collective-permute-start.4) | collective-permute-done | bytes 163872 | tf_op jit(solution)/shard_map/ppermute | solution.py:266
  14.5 0.0 copy-done.9
  14.5 0.0 copy-done.8
  14.5 0.0 copy-done.5
  14.5 0.0 copy-done.7
  14.6 0.0 copy-done.3
  14.6 0.0 copy-done.4
  14.6 0.0 copy-done.6
  14.6 0.0 copy-done.2
  14.6 0.0 copy-done.1
  14.6 0.0 copy-done
  14.6 5.0 %crop.1 = bf16[64,128]{1,0:T(8,128)(2,1)} custom-call(bf16[8,80,128]{2,1,0:T(8,128)(2,1)S(1)} %constant_dynamic-update-slice_fusion.here_ref, bf16[8,80,128]{2,1,0:T(8,128)(2,1)S(1)} %collective-permute-done.4.there_ref, f32[16,8,128]{2,1,0:T(8,128)S(1)} %pad.14.token_pair_ref, bf16[4,128,128]{2,1,0:T(8,128)(2,1)S(1)} %and_select_fusion.key_place_ref, ...), custom_call_target="tpu_custom_call" | custom-call | tf_op jit(solution)/shard_map/crop/pallas_call | solution.py:282
  (16 shorter events, 0.1 us)
Async XLA Ops:
  0.8 5.1 %collective-permute-start = (bf16[1,80,128]{2,1,0:T(8,128)(2,1)S(1)}, bf16[1,80,128]{2,1,0:T(8,128)(2,1)S(1)}, u32[]{:S(2)}, u32[]{:S(2)}) collective-permute-start(bf16[1,80,128]{2,1,0:T(8,128)(2,1)S(1)} %get-tuple-element.6), channel_id=1, source_target_pairs={{0,9},{1,8},{2,11},{3,10},{4,13},{5,12},{6,15},{7,14},{8,1},{9,0},... | collective-permute-start | bytes 61448 | tf_op jit(solution)/shard_map/ppermute | solution.py:266
  4.4 0.7 %copy-start.10 = (s32[32]{0:T(128)S(1)}, s32[32]{0:T(128)}, u32[]{:S(2)}) copy-start(s32[32]{0:T(128)} %param.15) | copy-start | bytes 388
  5.1 9.4 %copy-start.9 = (bf16[128,4]{0,1:T(4,128)(2,1)S(1)}, bf16[128,4]{0,1:T(4,128)(2,1)}, u32[]{:S(2)}) copy-start(bf16[128,4]{0,1:T(4,128)(2,1)} %param.21) | copy-start | bytes 3076
  5.2 9.4 %copy-start.8 = (bf16[128,128]{1,0:T(8,128)(2,1)S(1)}, bf16[128,128]{1,0:T(8,128)(2,1)}, u32[]{:S(2)}) copy-start(bf16[128,128]{1,0:T(8,128)(2,1)} %attn_outproj_ref.1) | copy-start | bytes 98308
  5.2 9.4 %copy-start.5 = (bf16[128,256]{1,0:T(8,128)(2,1)S(1)}, bf16[128,256]{1,0:T(8,128)(2,1)}, u32[]{:S(2)}) copy-start(bf16[128,256]{1,0:T(8,128)(2,1)} %mult_value_ref.1) | copy-start | bytes 196612
  5.2 9.4 %copy-start.7 = (bf16[128,128]{1,0:T(8,128)(2,1)S(1)}, bf16[128,128]{1,0:T(8,128)(2,1)}, u32[]{:S(2)}) copy-start(bf16[128,128]{1,0:T(8,128)(2,1)} %mult_outproj_ref.1) | copy-start | bytes 98308
  5.4 9.2 %copy-start.3 = (bf16[512,128]{1,0:T(8,128)(2,1)S(1)}, bf16[512,128]{1,0:T(8,128)(2,1)}, u32[]{:S(2)}) copy-start(bf16[512,128]{1,0:T(8,128)(2,1)} %trans_outproj_ref.1) | copy-start | bytes 393220
  5.9 8.7 %copy-start.4 = (bf16[128,256]{1,0:T(8,128)(2,1)S(1)}, bf16[128,256]{1,0:T(8,128)(2,1)}, u32[]{:S(2)}) copy-start(bf16[128,256]{1,0:T(8,128)(2,1)} %mult_gate_ref.1) | copy-start | bytes 196612
  5.9 3.6 %collective-permute-start.1 = (bf16[2,80,128]{2,1,0:T(8,128)(2,1)S(1)}, bf16[2,80,128]{2,1,0:T(8,128)(2,1)S(1)}, u32[]{:S(2)}, u32[]{:S(2)}) collective-permute-start(bf16[2,80,128]{2,1,0:T(8,128)(2,1)S(1)} %pad_maximum_fusion), channel_id=1, source_target_pairs={{0,5},{1,4},{2,7},{3,6},{4,1},{5,0},{6,3},{7,2},{8,13},{9,12},{10,... | collective-permute-start | bytes 122888 | tf_op jit(solution)/shard_map/ppermute | solution.py:266
  7.8 3.5 %collective-permute-start.2 = (bf16[2,80,128]{2,1,0:T(8,128)(2,1)S(1)}, bf16[2,80,128]{2,1,0:T(8,128)(2,1)S(1)}, u32[]{:S(2)}, u32[]{:S(2)}) collective-permute-start(bf16[2,80,128]{2,1,0:T(8,128)(2,1)S(1)} %pad_maximum_fusion), channel_id=1, source_target_pairs={{0,3},{1,2},{2,1},{3,0},{4,7},{5,6},{6,5},{7,4},{8,11},{9,10},{10,... | collective-permute-start | bytes 122888 | tf_op jit(solution)/shard_map/ppermute | solution.py:266
  9.3 5.2 %copy-start.6 = (bf16[128,128]{1,0:T(8,128)(2,1)S(1)}, bf16[128,128]{1,0:T(8,128)(2,1)}, u32[]{:S(2)}) copy-start(bf16[128,128]{1,0:T(8,128)(2,1)} %mult_outgate_ref.1) | copy-start | bytes 98308
  9.5 3.5 %collective-permute-start.3 = (bf16[2,80,128]{2,1,0:T(8,128)(2,1)S(1)}, bf16[2,80,128]{2,1,0:T(8,128)(2,1)S(1)}, u32[]{:S(2)}, u32[]{:S(2)}) collective-permute-start(bf16[2,80,128]{2,1,0:T(8,128)(2,1)S(1)} %collective-permute-done.1), channel_id=1, source_target_pairs={{0,3},{1,2},{2,1},{3,0},{4,7},{5,6},{6,5},{7,4},{8,11},{9,10},{10,... | collective-permute-start | bytes 122888 | tf_op jit(solution)/shard_map/ppermute | solution.py:266
  11.3 3.3 %copy-start.2 = (bf16[128,512]{1,0:T(8,128)(2,1)S(1)}, bf16[128,512]{1,0:T(8,128)(2,1)}, u32[]{:S(2)}) copy-start(bf16[128,512]{1,0:T(8,128)(2,1)} %trans_value_ref.1) | copy-start | bytes 393220
  11.3 3.3 %copy-start.1 = (bf16[128,512]{1,0:T(8,128)(2,1)S(1)}, bf16[128,512]{1,0:T(8,128)(2,1)}, u32[]{:S(2)}) copy-start(bf16[128,512]{1,0:T(8,128)(2,1)} %trans_gate_ref.1) | copy-start | bytes 393220
  11.4 3.2 %copy-start = (bf16[128,512]{1,0:T(8,128)(2,1)S(1)}, bf16[128,512]{1,0:T(8,128)(2,1)}, u32[]{:S(2)}) copy-start(bf16[128,512]{1,0:T(8,128)(2,1)} %attn_proj_ref.1) | copy-start | bytes 393220
  13.0 1.5 %collective-permute-start.4 = (bf16[8,80,128]{2,1,0:T(8,128)(2,1)S(1)}, bf16[8,80,128]{2,1,0:T(8,128)(2,1)S(1)}, u32[]{:S(2)}, u32[]{:S(2)}) collective-permute-start(bf16[8,80,128]{2,1,0:T(8,128)(2,1)S(1)} %constant_dynamic-update-slice_fusion.here_ref), channel_id=1, source_target_pairs={{0,1},{1,0},{2,3},{3,2},{4,5},{5,4},{6,7},{7,6},{8,9},{9,8},{10,11... | collective-permute-start | bytes 491528 | tf_op jit(solution)/shard_map/ppermute | solution.py:266

commit v5 on v4

--- a/solution.py
+++ b/solution.py
@@ -91,16 +91,6 @@
         lax.broadcasted_iota(jnp.int32, (block_cols, lanes), 0)
         == lax.broadcasted_iota(jnp.int32, (block_cols, lanes), 1)
     ).astype(jnp.float32)
-    head_lanes = (
-        lax.broadcasted_iota(jnp.int32, (heads, spans), 0)
-        == lax.broadcasted_iota(jnp.int32, (heads, spans), 1) // length
-    ).astype(jnp.float32)
-    bias_wide_ref[...] = lax.dot_general(
-        attn_bias_ref[...].astype(jnp.float32),
-        head_lanes,
-        (((0,), (0,)), ((), ())),
-        preferred_element_type=jnp.float32,
-    ).astype(jnp.bfloat16)
     masks = []
     for slot, offset in enumerate(slots):
         half_ref = (here_ref, there_ref)[slot // (devices // 2)]
@@ -116,6 +106,27 @@
             start = slot * pairs + row * block_cols
             right[pl.ds(slot * pairs + row, block_cols, stride=block_rows), :] = turned[start : start + block_cols]
 
+    first_row = me * own_rows
+    part = first_row // block_rows
+    first_own = first_row - part * block_rows
+    own_pairs = own_rows * block_cols
+    inside = pl.ds(pl.multiple_of(first_own * block_cols, own_pairs), own_pairs)
+    own_slots = [slot_at(part, col) for col in range(col_count)]
+    key_mask = jnp.zeros(key_lane.shape, jnp.float32)
+    for col in range(col_count):
+        mask = crop_ref[own_slots[col], pairs:, :]
+        key_mask = key_mask + dot(mask, key_place_ref[col])
+    key_lane[...] = key_mask
+    head_lanes = (
+        lax.broadcasted_iota(jnp.int32, (heads, spans), 0)
+        == lax.broadcasted_iota(jnp.int32, (heads, spans), 1) // length
+    ).astype(jnp.float32)
+    bias_wide_ref[...] = lax.dot_general(
+        attn_bias_ref[...].astype(jnp.float32),
+        head_lanes,
+        (((0,), (0,)), ((), ())),
+        preferred_element_type=jnp.float32,
+    ).astype(jnp.bfloat16)
     starts = [[slot_at(row, col) * pairs for col in range(col_count)] for row in range(row_count)]
 
     for part in range(row_count):
@@ -151,13 +162,6 @@
         rows = track + gate * dot(mixed, mult_outproj_ref[...])
         return rows, layer_norm(rows).astype(jnp.bfloat16)
 
-    first_row = me * own_rows
-    part = first_row // block_rows
-    first_own = first_row - part * block_rows
-    own_pairs = own_rows * block_cols
-    inside = pl.ds(pl.multiple_of(first_own * block_cols, own_pairs), own_pairs)
-    own_slots = [slot_at(part, col) for col in range(col_count)]
-
     def own_block(values):
         values = [value.reshape(own_rows, block_cols, channels) for value in values]
         return jnp.concatenate(values, axis=1).reshape(own_rows * length, channels)
@@ -177,11 +181,6 @@
     keys = projected[:, inner : 2 * inner]
     values = projected[:, 2 * inner : 3 * inner]
     gating = sigmoid(projected[:, 3 * inner :])
-    key_mask = jnp.zeros(key_lane.shape, jnp.float32)
-    for col in range(col_count):
-        mask = crop_ref[own_slots[col], pairs:, :]
-        key_mask = key_mask + dot(mask, key_place_ref[col])
-    key_lane[...] = key_mask
     head_of_lane = lax.broadcasted_iota(jnp.int32, (1, spans), 1) // length
     head_of_row = lax.broadcasted_iota(jnp.int32, (spans, inner), 0) // length
     head_of_channel = lax.broadcasted_iota(jnp.int32, (spans, inner), 1) // head_width

time: 19.8 us -> 19.2 us (0.970)
  Pallas kernels: 4.95 us -> 4.35 us
    pallas_call x1, Pallas kernels: 4.95 us -> 4.35 us  [gathered_crop(): pl.pallas_call(functools.partial(crop_kernel, tuple(slots), col_count), o...]
where the time goes in v5:
time: 19.2 us; the launch traced here: 19 us
  starting transfers between devices  9.3 us (48%)
  Pallas kernels  4.35 us (23%)
  waiting for transfers between devices  3.23 us (17%)
  other arithmetic  0.98 us (5%)
  local copies, waits for them, and re-layouts  0.92 us (5%)
    ppermute x5, starting transfers between devices, gathered_crop(): lax.ppermute(part, crop_axes, pairing)  9.3 us
    pallas_call x1, Pallas kernels, gathered_crop(): pl.pallas_call(functools.partial(crop_kernel, tuple(slots), col_count), o...  4.35 us
    ppermute x5, waiting for transfers between devices, gathered_crop(): lax.ppermute(part, crop_axes, pairing)  3.23 us
    unnamed x1, other arithmetic  0.81 us
    unnamed x25, local copies, waits for them, and re-layouts  0.73 us
  transfers between devices with their start and end apart: 5, of which 4 were waited for; matrix products, arithmetic and copies ran while one was open for 2% of the time, Pallas kernels for 0%

profile of v5, /device:TPU:0, one launch (start us, length us, event | category | flops | bytes accessed | tf_op | source)
XLA Modules:
  0.0 19.0 jit_solution(6033999695922589381)
XLA Ops:
  0.0 0.8 %constant_dynamic-update-slice_fusion.4 = (bf16[8,80,128]{2,1,0:T(8,128)(2,1)S(1)}, bf16[1,80,128]{2,1,0:T(8,128)(2,1)S(1)}) fusion(s32[8,8]{1,0:T(8,128)} %param.14, bf16[64,128]{1,0:T(8,128)(2,1)} %bitcast.11, pred[80]{0:T(512)(128)(4,1)S(1)} %iota_compare_fusion.2), kind=kLoop, calls=%fused_computation.12 | loop fusion | flops 40959 | bytes 57680
  0.8 3.5 %collective-permute-start = (bf16[1,80,128]{2,1,0:T(8,128)(2,1)S(1)}, bf16[1,80,128]{2,1,0:T(8,128)(2,1)S(1)}, u32[]{:S(2)}, u32[]{:S(2)}) collective-permute-start(bf16[1,80,128]{2,1,0:T(8,128)(2,1)S(1)} %get-tuple-element.6), channel_id=1, source_target_pairs={{0,9},{1,8},{2,11},{3,10},{4,13},{5,12},{6,15},{7,14},{8,1},{9,0},... | collective-permute-start | bytes 61448 | tf_op jit(solution)/shard_map/ppermute | solution.py:265
  4.4 0.0 copy-start.10
  4.4 0.6 %copy-done.10 = s32[32]{0:T(128)S(1)} copy-done((s32[32]{0:T(128)S(1)}, s32[32]{0:T(128)}, u32[]{:S(2)}) %copy-start.10) | copy-done | bytes 152
  5.0 0.1 mul.32
  5.1 0.0 copy-start.9
  5.2 0.0 copy-start.8
  5.2 0.0 copy-start.5
  5.2 0.0 copy-start.7
  5.2 0.1 broadcast_multiply_fusion
  5.3 0.1 convert_element_type.25
  5.4 0.0 copy-start.3
  5.4 0.5 %collective-permute-done = bf16[1,80,128]{2,1,0:T(8,128)(2,1)S(1)} collective-permute-done((bf16[1,80,128]{2,1,0:T(8,128)(2,1)S(1)}, bf16[1,80,128]{2,1,0:T(8,128)(2,1)S(1)}, u32[]{:S(2)}, u32[]{:S(2)}) %collective-permute-start) | collective-permute-done | bytes 20512 | tf_op jit(solution)/shard_map/ppermute | solution.py:265
  5.9 0.0 copy-start.4
  5.9 1.9 %collective-permute-start.1 = (bf16[2,80,128]{2,1,0:T(8,128)(2,1)S(1)}, bf16[2,80,128]{2,1,0:T(8,128)(2,1)S(1)}, u32[]{:S(2)}, u32[]{:S(2)}) collective-permute-start(bf16[2,80,128]{2,1,0:T(8,128)(2,1)S(1)} %pad_maximum_fusion), channel_id=1, source_target_pairs={{0,5},{1,4},{2,7},{3,6},{4,1},{5,0},{6,3},{7,2},{8,13},{9,12},{10,... | collective-permute-start | bytes 122888 | tf_op jit(solution)/shard_map/ppermute | solution.py:265
  7.8 1.5 %collective-permute-start.2 = (bf16[2,80,128]{2,1,0:T(8,128)(2,1)S(1)}, bf16[2,80,128]{2,1,0:T(8,128)(2,1)S(1)}, u32[]{:S(2)}, u32[]{:S(2)}) collective-permute-start(bf16[2,80,128]{2,1,0:T(8,128)(2,1)S(1)} %pad_maximum_fusion), channel_id=1, source_target_pairs={{0,3},{1,2},{2,1},{3,0},{4,7},{5,6},{6,5},{7,4},{8,11},{9,10},{10,... | collective-permute-start | bytes 122888 | tf_op jit(solution)/shard_map/ppermute | solution.py:265
  9.3 0.0 copy-start.6
  9.4 0.2 collective-permute-done.1
  9.5 1.8 %collective-permute-start.3 = (bf16[2,80,128]{2,1,0:T(8,128)(2,1)S(1)}, bf16[2,80,128]{2,1,0:T(8,128)(2,1)S(1)}, u32[]{:S(2)}, u32[]{:S(2)}) collective-permute-start(bf16[2,80,128]{2,1,0:T(8,128)(2,1)S(1)} %collective-permute-done.1), channel_id=1, source_target_pairs={{0,3},{1,2},{2,1},{3,0},{4,7},{5,6},{6,5},{7,4},{8,11},{9,10},{10,... | collective-permute-start | bytes 122888 | tf_op jit(solution)/shard_map/ppermute | solution.py:265
  11.3 0.0 copy-start.2
  11.3 0.0 collective-permute-done.2
  11.3 0.0 copy-start.1
  11.4 0.0 copy-start
  11.4 1.6 %collective-permute-done.3 = bf16[2,80,128]{2,1,0:T(8,128)(2,1)S(1)} collective-permute-done((bf16[2,80,128]{2,1,0:T(8,128)(2,1)S(1)}, bf16[2,80,128]{2,1,0:T(8,128)(2,1)S(1)}, u32[]{:S(2)}, u32[]{:S(2)}) %collective-permute-start.3) | collective-permute-done | bytes 40992 | tf_op jit(solution)/shard_map/ppermute | solution.py:265
  13.0 0.5 %collective-permute-start.4 = (bf16[8,80,128]{2,1,0:T(8,128)(2,1)S(1)}, bf16[8,80,128]{2,1,0:T(8,128)(2,1)S(1)}, u32[]{:S(2)}, u32[]{:S(2)}) collective-permute-start(bf16[8,80,128]{2,1,0:T(8,128)(2,1)S(1)} %constant_dynamic-update-slice_fusion.here_ref), channel_id=1, source_target_pairs={{0,1},{1,0},{2,3},{3,2},{4,5},{5,4},{6,7},{7,6},{8,9},{9,8},{10,11... | collective-permute-start | bytes 491528 | tf_op jit(solution)/shard_map/ppermute | solution.py:265
  13.6 1.0 %collective-permute-done.4.there_ref = bf16[8,80,128]{2,1,0:T(8,128)(2,1)S(1)} collective-permute-done((bf16[8,80,128]{2,1,0:T(8,128)(2,1)S(1)}, bf16[8,80,128]{2,1,0:T(8,128)(2,1)S(1)}, u32[]{:S(2)}, u32[]{:S(2)}) %collective-permute-start.4) | collective-permute-done | bytes 163872 | tf_op jit(solution)/shard_map/ppermute | solution.py:265
  14.5 0.0 copy-done.9
  14.5 0.0 copy-done.8
  14.5 0.0 copy-done.5
  14.5 0.0 copy-done.7
  14.6 0.0 copy-done.3
  14.6 0.0 copy-done.4
  14.6 0.0 copy-done.6
  14.6 0.0 copy-done.2
  14.6 0.0 copy-done.1
  14.6 0.0 copy-done
  14.6 4.3 %crop.1 = bf16[64,128]{1,0:T(8,128)(2,1)} custom-call(bf16[8,80,128]{2,1,0:T(8,128)(2,1)S(1)} %constant_dynamic-update-slice_fusion.here_ref, bf16[8,80,128]{2,1,0:T(8,128)(2,1)S(1)} %collective-permute-done.4.there_ref, f32[16,8,128]{2,1,0:T(8,128)S(1)} %pad.14.token_pair_ref, bf16[4,128,128]{2,1,0:T(8,128)(2,1)S(1)} %and_select_fusion.key_place_ref, ...), custom_call_target="tpu_custom_call" | custom-call | tf_op jit(solution)/shard_map/crop/pallas_call | solution.py:281
  (16 shorter events, 0.1 us)
Async XLA Ops:
  0.8 5.1 %collective-permute-start = (bf16[1,80,128]{2,1,0:T(8,128)(2,1)S(1)}, bf16[1,80,128]{2,1,0:T(8,128)(2,1)S(1)}, u32[]{:S(2)}, u32[]{:S(2)}) collective-permute-start(bf16[1,80,128]{2,1,0:T(8,128)(2,1)S(1)} %get-tuple-element.6), channel_id=1, source_target_pairs={{0,9},{1,8},{2,11},{3,10},{4,13},{5,12},{6,15},{7,14},{8,1},{9,0},... | collective-permute-start | bytes 61448 | tf_op jit(solution)/shard_map/ppermute | solution.py:265
  4.4 0.7 %copy-start.10 = (s32[32]{0:T(128)S(1)}, s32[32]{0:T(128)}, u32[]{:S(2)}) copy-start(s32[32]{0:T(128)} %param.15) | copy-start | bytes 388
  5.1 9.4 %copy-start.9 = (bf16[128,4]{0,1:T(4,128)(2,1)S(1)}, bf16[128,4]{0,1:T(4,128)(2,1)}, u32[]{:S(2)}) copy-start(bf16[128,4]{0,1:T(4,128)(2,1)} %param.21) | copy-start | bytes 3076
  5.2 9.4 %copy-start.8 = (bf16[128,128]{1,0:T(8,128)(2,1)S(1)}, bf16[128,128]{1,0:T(8,128)(2,1)}, u32[]{:S(2)}) copy-start(bf16[128,128]{1,0:T(8,128)(2,1)} %attn_outproj_ref.1) | copy-start | bytes 98308
  5.2 9.4 %copy-start.5 = (bf16[128,256]{1,0:T(8,128)(2,1)S(1)}, bf16[128,256]{1,0:T(8,128)(2,1)}, u32[]{:S(2)}) copy-start(bf16[128,256]{1,0:T(8,128)(2,1)} %mult_value_ref.1) | copy-start | bytes 196612
  5.2 9.4 %copy-start.7 = (bf16[128,128]{1,0:T(8,128)(2,1)S(1)}, bf16[128,128]{1,0:T(8,128)(2,1)}, u32[]{:S(2)}) copy-start(bf16[128,128]{1,0:T(8,128)(2,1)} %mult_outproj_ref.1) | copy-start | bytes 98308
  5.4 9.2 %copy-start.3 = (bf16[512,128]{1,0:T(8,128)(2,1)S(1)}, bf16[512,128]{1,0:T(8,128)(2,1)}, u32[]{:S(2)}) copy-start(bf16[512,128]{1,0:T(8,128)(2,1)} %trans_outproj_ref.1) | copy-start | bytes 393220
  5.9 8.7 %copy-start.4 = (bf16[128,256]{1,0:T(8,128)(2,1)S(1)}, bf16[128,256]{1,0:T(8,128)(2,1)}, u32[]{:S(2)}) copy-start(bf16[128,256]{1,0:T(8,128)(2,1)} %mult_gate_ref.1) | copy-start | bytes 196612
  5.9 3.6 %collective-permute-start.1 = (bf16[2,80,128]{2,1,0:T(8,128)(2,1)S(1)}, bf16[2,80,128]{2,1,0:T(8,128)(2,1)S(1)}, u32[]{:S(2)}, u32[]{:S(2)}) collective-permute-start(bf16[2,80,128]{2,1,0:T(8,128)(2,1)S(1)} %pad_maximum_fusion), channel_id=1, source_target_pairs={{0,5},{1,4},{2,7},{3,6},{4,1},{5,0},{6,3},{7,2},{8,13},{9,12},{10,... | collective-permute-start | bytes 122888 | tf_op jit(solution)/shard_map/ppermute | solution.py:265
  7.8 3.5 %collective-permute-start.2 = (bf16[2,80,128]{2,1,0:T(8,128)(2,1)S(1)}, bf16[2,80,128]{2,1,0:T(8,128)(2,1)S(1)}, u32[]{:S(2)}, u32[]{:S(2)}) collective-permute-start(bf16[2,80,128]{2,1,0:T(8,128)(2,1)S(1)} %pad_maximum_fusion), channel_id=1, source_target_pairs={{0,3},{1,2},{2,1},{3,0},{4,7},{5,6},{6,5},{7,4},{8,11},{9,10},{10,... | collective-permute-start | bytes 122888 | tf_op jit(solution)/shard_map/ppermute | solution.py:265
  9.3 5.2 %copy-start.6 = (bf16[128,128]{1,0:T(8,128)(2,1)S(1)}, bf16[128,128]{1,0:T(8,128)(2,1)}, u32[]{:S(2)}) copy-start(bf16[128,128]{1,0:T(8,128)(2,1)} %mult_outgate_ref.1) | copy-start | bytes 98308
  9.5 3.5 %collective-permute-start.3 = (bf16[2,80,128]{2,1,0:T(8,128)(2,1)S(1)}, bf16[2,80,128]{2,1,0:T(8,128)(2,1)S(1)}, u32[]{:S(2)}, u32[]{:S(2)}) collective-permute-start(bf16[2,80,128]{2,1,0:T(8,128)(2,1)S(1)} %collective-permute-done.1), channel_id=1, source_target_pairs={{0,3},{1,2},{2,1},{3,0},{4,7},{5,6},{6,5},{7,4},{8,11},{9,10},{10,... | collective-permute-start | bytes 122888 | tf_op jit(solution)/shard_map/ppermute | solution.py:265
  11.3 3.3 %copy-start.2 = (bf16[128,512]{1,0:T(8,128)(2,1)S(1)}, bf16[128,512]{1,0:T(8,128)(2,1)}, u32[]{:S(2)}) copy-start(bf16[128,512]{1,0:T(8,128)(2,1)} %trans_value_ref.1) | copy-start | bytes 393220
  11.3 3.3 %copy-start.1 = (bf16[128,512]{1,0:T(8,128)(2,1)S(1)}, bf16[128,512]{1,0:T(8,128)(2,1)}, u32[]{:S(2)}) copy-start(bf16[128,512]{1,0:T(8,128)(2,1)} %trans_gate_ref.1) | copy-start | bytes 393220
  11.4 3.2 %copy-start = (bf16[128,512]{1,0:T(8,128)(2,1)S(1)}, bf16[128,512]{1,0:T(8,128)(2,1)}, u32[]{:S(2)}) copy-start(bf16[128,512]{1,0:T(8,128)(2,1)} %attn_proj_ref.1) | copy-start | bytes 393220
  13.0 1.5 %collective-permute-start.4 = (bf16[8,80,128]{2,1,0:T(8,128)(2,1)S(1)}, bf16[8,80,128]{2,1,0:T(8,128)(2,1)S(1)}, u32[]{:S(2)}, u32[]{:S(2)}) collective-permute-start(bf16[8,80,128]{2,1,0:T(8,128)(2,1)S(1)} %constant_dynamic-update-slice_fusion.here_ref), channel_id=1, source_target_pairs={{0,1},{1,0},{2,3},{3,2},{4,5},{5,4},{6,7},{7,6},{8,9},{9,8},{10,11... | collective-permute-start | bytes 491528 | tf_op jit(solution)/shard_map/ppermute | solution.py:265
